TPU v7x, 32 devices: a whole 2x2x4 slice. The times are simulated.
32 devices in a mesh: blk: 8 (over y, x, core), seq: 4 (over z).
Axes of the slice: x: 2, y: 2, z: 4, core: 2. Of those that a mesh axis runs over, the one named last changes fastest.
Arguments:
- tokens: bfloat16 [64, 512, 768], P('blk', 'seq'), may hold values from -6 to 6
- lengths: int32 [64, 4], P('blk'), may hold values from 1 to 509, as said below
- pair_ids: int32 [128], P(('blk', 'seq')), may hold values from 0 to 127, each once
- w_query: bfloat16 [768, 768], P(('blk', 'seq')), may hold values from -0.21875 to 0.21875
- b_query: bfloat16 [768], P(('blk', 'seq')), may hold values from -1.75 to 1.75
- w_key: bfloat16 [768, 768], P(('blk', 'seq')), may hold values from -0.21875 to 0.21875
- w_value: bfloat16 [768, 768], P(('blk', 'seq')), may hold values from -0.21875 to 0.21875
- b_value: bfloat16 [768], P(('blk', 'seq')), may hold values from -1.75 to 1.75
- w_out: bfloat16 [768, 768], P(('blk', 'seq')), may hold values from -0.875 to 0.875
- b_out: bfloat16 [768], P(('blk', 'seq')), may hold values from -1.75 to 1.75
- norm1_gain: bfloat16 [768], P(('blk', 'seq')), may hold values from 0.5 to 1.5
- norm1_bias: bfloat16 [768], P(('blk', 'seq')), may hold values from -1.75 to 1.75
- w_in: bfloat16 [768, 3072], P(('blk', 'seq')), may hold values from -0.21875 to 0.21875
- b_in: bfloat16 [3072], P(('blk', 'seq')), may hold values from -1.75 to 1.75
- w_down: bfloat16 [3072, 768], P(('blk', 'seq')), may hold values from -0.109375 to 0.109375
- b_down: bfloat16 [768], P(('blk', 'seq')), may hold values from -1.75 to 1.75
- norm2_gain: bfloat16 [768], P(('blk', 'seq')), may hold values from 0.5 to 1.5
- norm2_bias: bfloat16 [768], P(('blk', 'seq')), may hold values from -0.75 to 0.75
Outputs:
- hidden_out: bfloat16 [64, 512, 768], P('blk', 'seq')
- query_loss: float32 [128], P(('blk', 'seq'))
- grad_tokens: float32 [64, 512, 768], P('blk', 'seq')
- grad_w_query: float32 [768, 768], P(('blk', 'seq'))
- grad_b_query: float32 [768], P(('blk', 'seq'))
- grad_w_key: float32 [768, 768], P(('blk', 'seq'))
- grad_w_value: float32 [768, 768], P(('blk', 'seq'))
- grad_b_value: float32 [768], P(('blk', 'seq'))
- grad_w_out: float32 [768, 768], P(('blk', 'seq'))
- grad_b_out: float32 [768], P(('blk', 'seq'))
- grad_norm1_gain: float32 [768], P(('blk', 'seq'))
- grad_norm1_bias: float32 [768], P(('blk', 'seq'))
- grad_w_in: float32 [768, 3072], P(('blk', 'seq'))
- grad_b_in: float32 [3072], P(('blk', 'seq'))
- grad_w_down: float32 [3072, 768], P(('blk', 'seq'))
- grad_b_down: float32 [768], P(('blk', 'seq'))
- grad_norm2_gain: float32 [768], P(('blk', 'seq'))
- grad_norm2_bias: float32 [768], P(('blk', 'seq'))
Inputs may be any that keep to these rules, and one draw needn't show every extreme that they name: `lengths`: in each row one segment, at a place drawn from the seed, covers all but at most 127 of the row's tokens; the others have 1 to 32 tokens; fewer than 32 tokens at the row's end are padding. `pair_ids`: each document is paired with exactly one query.
All inputs are finite; a program needn't handle non-finite values.
Results may differ from a plain program's by a relative error of at most 0.015.
Values may be sent and summed in bfloat16 or wider, within the bound.
A program may use at most 256 MiB of HBM per device.

v0:
```python
import jax
import jax.numpy as jnp
from jax import lax
from jax.sharding import PartitionSpec as P

HEADS = 12
HEAD_DIM = 64
NQ = 2
SEGS = 4


SOFTMAX_WARMTH = 0.05
NORM_EPSILON = 1e-06
MASKED = -1000000000.0
MATMUL_EXACTNESS = lax.Precision.HIGHEST


def segment_ids(lengths, positions):
    ends = jnp.cumsum(lengths, axis=1)
    return jnp.sum((positions[None, :, None] >= ends[:, None, :]).astype(jnp.int32), axis=-1)


def matmul(operand, matrix):
    return jnp.einsum("rtd,de->rte", operand, matrix, preferred_element_type=jnp.float32)


def matmul_back(gradient, matrix):
    return jnp.einsum("rte,de->rtd", gradient, matrix, preferred_element_type=jnp.float32)


def outer_sum(operand, gradient):
    return jnp.einsum("rtd,rte->de", operand, gradient, preferred_element_type=jnp.float32)


def column_sum(gradient):
    return jnp.sum(gradient.astype(jnp.float32), axis=(0, 1))


def normalize(summed_in, gain_vec, shift_vec):
    center = summed_in - jnp.mean(summed_in, axis=-1, keepdims=True)
    inv_std = lax.rsqrt(jnp.mean(center * center, axis=-1, keepdims=True) + NORM_EPSILON)
    normed = center * inv_std
    return (normed * gain_vec.astype(jnp.float32) + shift_vec.astype(jnp.float32), normed, inv_std)


def normalize_back(gradient, normed, inv_std, gain_vec):
    scaled = gradient * gain_vec.astype(jnp.float32)
    return inv_std * (
        scaled
        - jnp.mean(scaled, axis=-1, keepdims=True)
        - normed * jnp.mean(scaled * normed, axis=-1, keepdims=True)
    )


def split_heads(tensor):
    return tensor.reshape(tensor.shape[0], tensor.shape[1], HEADS, HEAD_DIM)


def join_heads(tensor):
    return tensor.reshape(tensor.shape[0], tensor.shape[1], HEADS * HEAD_DIM)


def exact_gelu(tensor):
    return jax.nn.gelu(tensor, approximate=False)


def head_scores(queries, keys_all, allowed):
    scores = jnp.einsum(
        "rqhd,rkhd->rhqk",
        split_heads(queries),
        split_heads(keys_all),
        preferred_element_type=jnp.float32,
    ) * HEAD_DIM ** (-0.5)
    return jnp.where(allowed[:, None], scores, MASKED)


def layer_forward(weights, block_tokens, allowed, widen):
    (
        w_query,
        b_query,
        w_key,
        w_value,
        b_value,
        w_out,
        b_out,
        gain_one,
        shift_one,
        w_in,
        b_in,
        w_down,
        b_down,
        gain_two,
        shift_two,
    ) = weights
    queries = (matmul(block_tokens, w_query) + b_query.astype(jnp.float32)).astype(jnp.bfloat16)
    keys_local = matmul(block_tokens, w_key).astype(jnp.bfloat16)
    values_local = (matmul(block_tokens, w_value) + b_value.astype(jnp.float32)).astype(
        jnp.bfloat16
    )
    keys_all, values_all = widen(keys_local, values_local)
    scores = head_scores(queries, keys_all, allowed)
    log_total = jax.nn.logsumexp(scores, axis=-1, keepdims=True)
    softmax_low = jnp.exp(scores - log_total).astype(jnp.bfloat16)
    mixed = jnp.einsum(
        "rhqk,rkhd->rqhd", softmax_low, split_heads(values_all), preferred_element_type=jnp.float32
    )
    attended = join_heads(mixed).astype(jnp.bfloat16)
    pre_one = block_tokens.astype(jnp.float32) + matmul(attended, w_out) + b_out.astype(jnp.float32)
    hidden_one, normed_one, inv_one = normalize(pre_one, gain_one, shift_one)
    hidden_low = hidden_one.astype(jnp.bfloat16)
    inner_pre = matmul(hidden_low, w_in) + b_in.astype(jnp.float32)
    activated = exact_gelu(inner_pre).astype(jnp.bfloat16)
    pre_two = hidden_one + matmul(activated, w_down) + b_down.astype(jnp.float32)
    hidden_two, normed_two, inv_two = normalize(pre_two, gain_two, shift_two)
    stored = (
        queries,
        keys_all,
        values_all,
        log_total,
        attended,
        normed_one,
        inv_one,
        hidden_low,
        inner_pre,
        activated,
        normed_two,
        inv_two,
    )
    return (hidden_two, stored)


def layer_backward(weights, block_tokens, allowed, stored, grad_two, narrow):
    (
        w_query,
        b_query,
        w_key,
        w_value,
        b_value,
        w_out,
        b_out,
        gain_one,
        shift_one,
        w_in,
        b_in,
        w_down,
        b_down,
        gain_two,
        shift_two,
    ) = weights
    (
        queries,
        keys_all,
        values_all,
        log_total,
        attended,
        normed_one,
        inv_one,
        hidden_low,
        inner_pre,
        activated,
        normed_two,
        inv_two,
    ) = stored
    grad_gain_two = jnp.sum(grad_two * normed_two, axis=(0, 1))
    grad_shift_two = jnp.sum(grad_two, axis=(0, 1))
    grad_pre_two = normalize_back(grad_two, normed_two, inv_two, gain_two)
    grad_feed = grad_pre_two.astype(jnp.bfloat16)
    grad_w_down = outer_sum(activated, grad_feed)
    grad_b_down = column_sum(grad_feed)
    grad_act = matmul_back(grad_feed, w_down)
    _, gelu_back = jax.vjp(exact_gelu, inner_pre)
    grad_inner = gelu_back(grad_act)[0].astype(jnp.bfloat16)
    grad_w_in = outer_sum(hidden_low, grad_inner)
    grad_b_in = column_sum(grad_inner)
    grad_hidden_one = grad_pre_two + matmul_back(grad_inner, w_in)
    grad_gain_one = jnp.sum(grad_hidden_one * normed_one, axis=(0, 1))
    grad_shift_one = jnp.sum(grad_hidden_one, axis=(0, 1))
    grad_pre_one = normalize_back(grad_hidden_one, normed_one, inv_one, gain_one)
    grad_branch = grad_pre_one.astype(jnp.bfloat16)
    grad_w_out = outer_sum(attended, grad_branch)
    grad_b_out = column_sum(grad_branch)
    grad_attended = split_heads(matmul_back(grad_branch, w_out).astype(jnp.bfloat16))
    scores = head_scores(queries, keys_all, allowed)
    softmax_w = jnp.exp(scores - log_total)
    softmax_low = softmax_w.astype(jnp.bfloat16)
    grad_values_all = join_heads(
        jnp.einsum(
            "rhqk,rqhd->rkhd", softmax_low, grad_attended, preferred_element_type=jnp.float32
        )
    )
    grad_softmax = jnp.einsum(
        "rqhd,rkhd->rhqk",
        grad_attended,
        split_heads(values_all),
        preferred_element_type=jnp.float32,
    )
    grad_scores = (
        softmax_w * (grad_softmax - jnp.sum(softmax_w * grad_softmax, axis=-1, keepdims=True))
    ).astype(jnp.bfloat16)
    grad_queries = (
        join_heads(
            jnp.einsum(
                "rhqk,rkhd->rqhd",
                grad_scores,
                split_heads(keys_all),
                preferred_element_type=jnp.float32,
            )
        )
        * HEAD_DIM ** (-0.5)
    ).astype(jnp.bfloat16)
    grad_keys_all = join_heads(
        jnp.einsum(
            "rhqk,rqhd->rkhd", grad_scores, split_heads(queries), preferred_element_type=jnp.float32
        )
    ) * HEAD_DIM ** (-0.5)
    grad_keys, grad_values = narrow(grad_keys_all, grad_values_all)
    grad_keys = grad_keys.astype(jnp.bfloat16)
    grad_values = grad_values.astype(jnp.bfloat16)
    grad_w_query = outer_sum(block_tokens, grad_queries)
    grad_b_query = column_sum(grad_queries)
    grad_w_key = outer_sum(block_tokens, grad_keys)
    grad_w_value = outer_sum(block_tokens, grad_values)
    grad_b_value = column_sum(grad_values)
    grad_block = (
        grad_pre_one
        + matmul_back(grad_queries, w_query)
        + matmul_back(grad_keys, w_key)
        + matmul_back(grad_values, w_value)
    )
    gradients = (
        grad_w_query,
        grad_b_query,
        grad_w_key,
        grad_w_value,
        grad_b_value,
        grad_w_out,
        grad_b_out,
        grad_gain_one,
        grad_shift_one,
        grad_w_in,
        grad_b_in,
        grad_w_down,
        grad_b_down,
        grad_gain_two,
        grad_shift_two,
    )
    return (grad_block, gradients)


def keys_gathered(keys_local, values_local):
    return (
        lax.all_gather(keys_local, "seq", axis=1, tiled=True),
        lax.all_gather(values_local, "seq", axis=1, tiled=True),
    )


def keys_summed(grad_keys_all, grad_values_all):
    return (
        lax.psum_scatter(
            grad_keys_all.astype(jnp.bfloat16), "seq", scatter_dimension=1, tiled=True
        ).astype(jnp.float32),
        lax.psum_scatter(
            grad_values_all.astype(jnp.bfloat16), "seq", scatter_dimension=1, tiled=True
        ).astype(jnp.float32),
    )


def per_device(
    tokens,
    lengths,
    pair_ids,
    w_query,
    b_query,
    w_key,
    w_value,
    b_value,
    w_out,
    b_out,
    norm1_gain,
    norm1_bias,
    w_in,
    b_in,
    w_down,
    b_down,
    norm2_gain,
    norm2_bias,
):
    shards = (
        w_query,
        b_query,
        w_key,
        w_value,
        b_value,
        w_out,
        b_out,
        norm1_gain,
        norm1_bias,
        w_in,
        b_in,
        w_down,
        b_down,
        norm2_gain,
        norm2_bias,
    )
    group_rows, local_len, width = tokens.shape
    seq_size = lax.axis_size("seq")
    seq_index = lax.axis_index("seq")
    own_rows = group_rows // seq_size
    own_lengths_int = lax.dynamic_slice_in_dim(lengths, seq_index * own_rows, own_rows, 0)
    key_segments = segment_ids(lengths, jnp.arange(local_len * seq_size, dtype=jnp.int32))
    query_segments = lax.dynamic_slice_in_dim(key_segments, seq_index * local_len, local_len, 1)
    row_count = tokens.shape[0]
    member_ids = jnp.arange(SEGS, dtype=jnp.int32)
    half_rows = row_count // 2
    stored_all = []
    allowed_all = []
    members_all = []
    pool_parts = []
    hidden_parts = []
    for batch_index in range(2):
        weights = (
            lax.all_gather(shards[0], ("blk", "seq"), axis=0, tiled=True),
            lax.all_gather(shards[1], ("blk", "seq"), axis=0, tiled=True),
            lax.all_gather(shards[2], ("blk", "seq"), axis=0, tiled=True),
            lax.all_gather(shards[3], ("blk", "seq"), axis=0, tiled=True),
            lax.all_gather(shards[4], ("blk", "seq"), axis=0, tiled=True),
            lax.all_gather(shards[5], ("blk", "seq"), axis=0, tiled=True),
            lax.all_gather(shards[6], ("blk", "seq"), axis=0, tiled=True),
            lax.all_gather(shards[7], ("blk", "seq"), axis=0, tiled=True),
            lax.all_gather(shards[8], ("blk", "seq"), axis=0, tiled=True),
            lax.all_gather(shards[9], ("blk", "seq"), axis=0, tiled=True),
            lax.all_gather(shards[10], ("blk", "seq"), axis=0, tiled=True),
            lax.all_gather(shards[11], ("blk", "seq"), axis=0, tiled=True),
            lax.all_gather(shards[12], ("blk", "seq"), axis=0, tiled=True),
            lax.all_gather(shards[13], ("blk", "seq"), axis=0, tiled=True),
            lax.all_gather(shards[14], ("blk", "seq"), axis=0, tiled=True),
        )
        first_row = batch_index * half_rows
        block_tokens = tokens[first_row : first_row + half_rows]
        block_query_seg = query_segments[first_row : first_row + half_rows]
        allowed = (
            block_query_seg[:, :, None]
            == key_segments[first_row : first_row + half_rows][:, None, :]
        )
        members = (block_query_seg[:, None, :] == member_ids[None, :, None]).astype(jnp.float32)
        hidden_two, stored = layer_forward(weights, block_tokens, allowed, keys_gathered)
        pool_parts.append(
            jnp.einsum("rsl,rld->rsd", members, hidden_two, precision=MATMUL_EXACTNESS)
        )
        hidden_parts.append(hidden_two.astype(jnp.bfloat16))
        stored_all.append(stored)
        allowed_all.append(allowed)
        members_all.append(members)
    pooled = lax.psum_scatter(
        jnp.concatenate(pool_parts, axis=0).astype(jnp.bfloat16),
        "seq",
        scatter_dimension=0,
        tiled=True,
    ).astype(jnp.float32)
    own_lengths = own_lengths_int.astype(jnp.float32)
    averaged = pooled / own_lengths[:, :, None]
    inv_norm = lax.rsqrt(jnp.sum(averaged * averaged, axis=-1, keepdims=True) + NORM_EPSILON)
    embedded = averaged * inv_norm
    query_count = own_rows * NQ
    query_vectors = embedded[:, :NQ].reshape(query_count, width)
    document_vectors = embedded[:, NQ:].reshape(query_count, width)
    start_max = jnp.full((query_count,), -1e30, jnp.float32)
    incoming = lax.all_gather(document_vectors, ("blk", "seq"), axis=0, tiled=True)
    similarity_scores = (
        jnp.einsum(
            "qd,kd->qk",
            query_vectors,
            incoming,
            precision=MATMUL_EXACTNESS,
            preferred_element_type=jnp.float32,
        )
        / SOFTMAX_WARMTH
    )
    doc_index = jnp.arange(incoming.shape[0], dtype=jnp.int32)
    positive = jnp.sum(
        jnp.where(pair_ids[:, None] == doc_index[None, :], similarity_scores, 0.0), axis=1
    )
    new_max = jnp.maximum(start_max, jnp.max(similarity_scores, axis=1))
    running_sum = jnp.sum(jnp.exp(similarity_scores - new_max[:, None]), axis=1)
    top_score, exponent_total, positive = (new_max, running_sum, positive)
    query_lse = top_score + jnp.log(exponent_total)
    query_loss = query_lse - positive
    own_docs = lax.axis_index(("blk", "seq")) * query_count + jnp.arange(
        query_count, dtype=jnp.int32
    )
    other_query = lax.all_gather(query_vectors, ("blk", "seq"), axis=0, tiled=True)
    other_lse = lax.all_gather(query_lse, ("blk", "seq"), axis=0, tiled=True)
    other_pair = lax.all_gather(pair_ids, ("blk", "seq"), axis=0, tiled=True)
    other_doc = lax.all_gather(document_vectors, ("blk", "seq"), axis=0, tiled=True)
    doc_index = jnp.arange(other_doc.shape[0], dtype=jnp.int32)
    forward_sim = (
        jnp.einsum(
            "qd,kd->qk",
            query_vectors,
            other_doc,
            precision=MATMUL_EXACTNESS,
            preferred_element_type=jnp.float32,
        )
        / SOFTMAX_WARMTH
    )
    forward_grad = jnp.exp(forward_sim - query_lse[:, None]) - (
        pair_ids[:, None] == doc_index[None, :]
    ).astype(jnp.float32)
    grad_query = (
        jnp.einsum(
            "qk,kd->qd",
            forward_grad,
            other_doc,
            precision=MATMUL_EXACTNESS,
            preferred_element_type=jnp.float32,
        )
        / SOFTMAX_WARMTH
    )
    reverse_sim = (
        jnp.einsum(
            "kd,jd->kj",
            other_query,
            document_vectors,
            precision=MATMUL_EXACTNESS,
            preferred_element_type=jnp.float32,
        )
        / SOFTMAX_WARMTH
    )
    reverse_grad = jnp.exp(reverse_sim - other_lse[:, None]) - (
        other_pair[:, None] == own_docs[None, :]
    ).astype(jnp.float32)
    grad_doc = (
        jnp.einsum(
            "kj,kd->jd",
            reverse_grad,
            other_query,
            precision=MATMUL_EXACTNESS,
            preferred_element_type=jnp.float32,
        )
        / SOFTMAX_WARMTH
    )
    grad_query, grad_doc = (grad_query, grad_doc)
    grad_emb = jnp.concatenate(
        (grad_query.reshape(own_rows, NQ, width), grad_doc.reshape(own_rows, NQ, width)), axis=1
    )
    grad_avg = inv_norm * grad_emb - inv_norm * inv_norm * inv_norm * averaged * jnp.sum(
        averaged * grad_emb, axis=-1, keepdims=True
    )
    grad_pools = lax.all_gather(grad_avg / own_lengths[:, :, None], "seq", axis=0, tiled=True)
    totals = None
    grad_parts = []
    for batch_index in range(2):
        weights = (
            lax.all_gather(shards[0], ("blk", "seq"), axis=0, tiled=True),
            lax.all_gather(shards[1], ("blk", "seq"), axis=0, tiled=True),
            lax.all_gather(shards[2], ("blk", "seq"), axis=0, tiled=True),
            lax.all_gather(shards[3], ("blk", "seq"), axis=0, tiled=True),
            lax.all_gather(shards[4], ("blk", "seq"), axis=0, tiled=True),
            lax.all_gather(shards[5], ("blk", "seq"), axis=0, tiled=True),
            lax.all_gather(shards[6], ("blk", "seq"), axis=0, tiled=True),
            lax.all_gather(shards[7], ("blk", "seq"), axis=0, tiled=True),
            lax.all_gather(shards[8], ("blk", "seq"), axis=0, tiled=True),
            lax.all_gather(shards[9], ("blk", "seq"), axis=0, tiled=True),
            lax.all_gather(shards[10], ("blk", "seq"), axis=0, tiled=True),
            lax.all_gather(shards[11], ("blk", "seq"), axis=0, tiled=True),
            lax.all_gather(shards[12], ("blk", "seq"), axis=0, tiled=True),
            lax.all_gather(shards[13], ("blk", "seq"), axis=0, tiled=True),
            lax.all_gather(shards[14], ("blk", "seq"), axis=0, tiled=True),
        )
        first_row = batch_index * half_rows
        grad_two = jnp.einsum(
            "rsl,rsd->rld",
            members_all[batch_index],
            grad_pools[first_row : first_row + half_rows],
            precision=MATMUL_EXACTNESS,
        )
        grad_block, gradients = layer_backward(
            weights,
            tokens[first_row : first_row + half_rows],
            allowed_all[batch_index],
            stored_all[batch_index],
            grad_two,
            keys_summed,
        )
        grad_parts.append(grad_block)
        totals = gradients if totals is None else jax.tree.map(jnp.add, totals, gradients)
    summed = lax.psum_scatter(totals, ("blk", "seq"), scatter_dimension=0, tiled=True)
    (
        grad_w_query,
        grad_b_query,
        grad_w_key,
        grad_w_value,
        grad_b_value,
        grad_w_out,
        grad_b_out,
        grad_gain_one,
        grad_shift_one,
        grad_w_in,
        grad_b_in,
        grad_w_down,
        grad_b_down,
        grad_gain_two,
        grad_shift_two,
    ) = summed
    hidden_out = jnp.concatenate(hidden_parts, axis=0)
    grad_tokens = jnp.concatenate(grad_parts, axis=0)
    return (
        hidden_out,
        query_loss,
        grad_tokens,
        grad_w_query,
        grad_b_query,
        grad_w_key,
        grad_w_value,
        grad_b_value,
        grad_w_out,
        grad_b_out,
        grad_gain_one,
        grad_shift_one,
        grad_w_in,
        grad_b_in,
        grad_w_down,
        grad_b_down,
        grad_gain_two,
        grad_shift_two,
    )


def solution(mesh):
    in_specs = (
        P("blk", "seq", None),
        P("blk", None),
        P(("blk", "seq")),
        P(("blk", "seq"), None),
        P(("blk", "seq")),
        P(("blk", "seq"), None),
        P(("blk", "seq"), None),
        P(("blk", "seq")),
        P(("blk", "seq"), None),
        P(("blk", "seq")),
        P(("blk", "seq")),
        P(("blk", "seq")),
        P(("blk", "seq"), None),
        P(("blk", "seq")),
        P(("blk", "seq"), None),
        P(("blk", "seq")),
        P(("blk", "seq")),
        P(("blk", "seq")),
    )
    out_specs = (
        P("blk", "seq", None),
        P(("blk", "seq")),
        P("blk", "seq", None),
        P(("blk", "seq"), None),
        P(("blk", "seq")),
        P(("blk", "seq"), None),
        P(("blk", "seq"), None),
        P(("blk", "seq")),
        P(("blk", "seq"), None),
        P(("blk", "seq")),
        P(("blk", "seq")),
        P(("blk", "seq")),
        P(("blk", "seq"), None),
        P(("blk", "seq")),
        P(("blk", "seq"), None),
        P(("blk", "seq")),
        P(("blk", "seq")),
        P(("blk", "seq")),
    )
    return jax.shard_map(
        per_device, mesh=mesh, in_specs=in_specs, out_specs=out_specs, check_vma=False
    )
```

profile of v0, /device:TPU:0, one launch (start us, length us, event | category | flops | bytes accessed | tf_op | source)
XLA Modules:
  0.0 1894.3 jit_solution(7915767341311028811)
XLA Ops:
  9.6 58.2 %all-gather.19.cloned.1.call-done = bf16[768,768]{1,0:T(8,128)(2,1)} async-done(((bf16[24,768]{1,0:T(8,128)(2,1)}), bf16[768,768]{1,0:T(8,128)(2,1)}) %all-gather.19.cloned.1.call-update) | async-done | bytes 1179664 | tf_op jit(solution)/shard_map/all_gather | solution.py:324
  73.2 39.7 %all-reduce.22 = (bf16[768]{0:T(1024)(128)(2,1)S(1)}, bf16[768]{0:T(1024)(128)(2,1)S(1)}, bf16[768]{0:T(1024)(128)(2,1)S(1)}, bf16[768]{0:T(1024)(128)(2,1)S(1)}...) all-reduce(bf16[768]{0:T(1024)(128)(2,1)S(1)} %dynamic-update-slice, ...), channel_id=1, replica_groups=mesh['blk'=8,'seq'=4] {'blk','seq'}, use_global_device_ids=true, to_apply=%add | all-reduce | flops 9216 | bytes 36864
  134.0 39.7 %all-reduce.10 = s32[128]{0:T(128)} all-reduce(s32[128]{0:T(128)S(1)} %dynamic-update-slice.10), channel_id=1, replica_groups=mesh['blk'=8,'seq'=4] {'blk','seq'}, use_global_device_ids=true, to_apply=%add.10 | all-reduce | flops 128 | bytes 1024
  186.2 58.1 %all-gather.21.cloned.1.call-done = bf16[4,512,768]{2,1,0:T(8,128)(2,1)} async-done(((bf16[4,128,768]{2,1,0:T(8,128)(2,1)}), bf16[4,512,768]{2,1,0:T(8,128)(2,1)}) %all-gather.21.cloned.1.call-update) | async-done | bytes 3145744 | tf_op jit(solution)/shard_map/all_gather | solution.py:252
  256.8 51.7 %all-gather.15.cloned.1.call-done = bf16[4,512,768]{2,1,0:T(8,128)(2,1)} async-done(((bf16[4,128,768]{2,1,0:T(8,128)(2,1)}), bf16[4,512,768]{2,1,0:T(8,128)(2,1)}) %all-gather.15.cloned.1.call-update) | async-done | bytes 3145744 | tf_op jit(solution)/shard_map/all_gather | solution.py:253
  322.2 41.8 %all-gather.23.cloned.1.call-done = bf16[768,768]{1,0:T(8,128)(2,1)} async-done(((bf16[24,768]{1,0:T(8,128)(2,1)}), bf16[768,768]{1,0:T(8,128)(2,1)}) %all-gather.23.cloned.1.call-update) | async-done | bytes 1179664 | tf_op jit(solution)/shard_map/all_gather | solution.py:327
  367.6 60.3 %all-gather.31.cloned.1.call-done = bf16[4,512,768]{2,1,0:T(8,128)(2,1)} async-done(((bf16[4,128,768]{2,1,0:T(8,128)(2,1)}), bf16[4,512,768]{2,1,0:T(8,128)(2,1)}) %all-gather.31.cloned.1.call-update) | async-done | bytes 3145744 | tf_op jit(solution)/shard_map/all_gather | solution.py:252
  440.2 51.5 %all-gather.29.cloned.1.call-done = bf16[4,512,768]{2,1,0:T(8,128)(2,1)} async-done(((bf16[4,128,768]{2,1,0:T(8,128)(2,1)}), bf16[4,512,768]{2,1,0:T(8,128)(2,1)}) %all-gather.29.cloned.1.call-update) | async-done | bytes 3145744 | tf_op jit(solution)/shard_map/all_gather | solution.py:253
  503.8 53.0 %all-gather.25.cloned.1.call-done = bf16[768,3072]{1,0:T(8,128)(2,1)} async-done(((bf16[24,3072]{1,0:T(8,128)(2,1)}), bf16[768,3072]{1,0:T(8,128)(2,1)}) %all-gather.25.cloned.1.call-update) | async-done | bytes 4718608 | tf_op jit(solution)/shard_map/all_gather | solution.py:331
  571.5 30.7 %multiply_convert_fusion.5 = (bf16[4,128,3072]{2,1,0:T(8,128)(2,1)}, f32[4,128,3072]{2,1,0:T(8,128)}, bf16[4,128,3072]{2,1,0:T(8,128)(2,1)}, f32[4,128,3072]{2,1,0:T(8,128)}) fusion(f32[4,128,3072]{2,1,0:T(8,128)S(1)} %get-tuple-element.177, f32[3072]{0:T(1024)S(1)} %convert_element_type.271, u8[128,3072]{1,0:T(8,128)(4,1)S(1)} %get-tuple-element.91, ...), kind=kLoop, calls=%fused_computation.49 | loop fusion | flops 221773824 | bytes 33042432 | tf_op jit(solution)/shard_map/convert_element_type | solution.py:112
  602.2 19.7 %all-gather.27.cloned.1.call-done = bf16[3072,768]{1,0:T(8,128)(2,1)} async-done(((bf16[96,768]{1,0:T(8,128)(2,1)}), bf16[3072,768]{1,0:T(8,128)(2,1)}) %all-gather.27.cloned.1.call-update) | async-done | bytes 4718608 | tf_op jit(solution)/shard_map/all_gather | solution.py:333
  633.6 18.9 all-reduce.11
  657.7 71.8 %all-gather.1 = f32[32,4,768]{2,1,0:T(4,128)} all-gather(f32[1,4,768]{2,1,0:T(4,128)} %reshape.309), channel_id=1, replica_groups=mesh['blk'=8,'seq'=4] {'blk','seq'}, dimensions={0}, use_global_device_ids=true | all-gather | bytes 405504 | tf_op jit(solution)/shard_map/all_gather | solution.py:391
  731.4 73.3 %all-gather = f32[32,4,768]{2,1,0:T(4,128)} all-gather(f32[1,4,768]{2,1,0:T(4,128)} %reshape.307), channel_id=1, replica_groups=mesh['blk'=8,'seq'=4] {'blk','seq'}, dimensions={0}, use_global_device_ids=true | all-gather | bytes 405504 | tf_op jit(solution)/shard_map/all_gather | solution.py:368
  811.6 38.3 %all-reduce.9 = f32[128]{0:T(128)S(1)} all-reduce(f32[128]{0:T(128)} %copy-done.133), channel_id=1, replica_groups=mesh['blk'=8,'seq'=4] {'blk','seq'}, use_global_device_ids=true, to_apply=%add.9 | all-reduce | flops 128 | bytes 1024
  1036.5 24.2 %reduce-scatter.33.cloned.1.call-done = bf16[128,3072]{1,0:T(8,128)(2,1)} async-done(((bf16[512,3072]{1,0:T(8,128)(2,1)}), bf16[128,3072]{1,0:T(8,128)(2,1)}) %reduce-scatter.33.cloned.1.call-update) | async-done | bytes 786448
  1071.8 51.5 %reduce-scatter.31.cloned.1.call-done = bf16[128,3072]{1,0:T(8,128)(2,1)} async-done(((bf16[512,3072]{1,0:T(8,128)(2,1)}), bf16[128,3072]{1,0:T(8,128)(2,1)}) %reduce-scatter.31.cloned.1.call-update) | async-done | bytes 786448
  1126.6 59.7 %reduce-scatter.35.cloned.1.call-done = bf16[128,3072]{1,0:T(8,128)(2,1)} async-done(((bf16[512,3072]{1,0:T(8,128)(2,1)}), bf16[128,3072]{1,0:T(8,128)(2,1)}) %reduce-scatter.35.cloned.1.call-update) | async-done | bytes 786448
  1227.2 41.7 %all-reduce.21 = (f32[768]{0:T(1024)S(1)}, f32[768]{0:T(1024)S(1)}, f32[768]{0:T(1024)S(1)}, f32[768]{0:T(1024)S(1)}, f32[768]{0:T(1024)S(1)}, /*index=5*/f32[30...) all-reduce(f32[768]{0:T(1024)S(1)} %add.365, ...), channel_id=8, replica_groups=mesh['blk'=8,'seq'=4] {'blk','seq'}, use_global_device_ids=true, to_apply=%region_37.38.clone | all-reduce | flops 9216 | bytes 73728
  1291.1 104.7 %reduce-scatter.39.cloned.1.call-done = f32[24,768]{1,0:T(8,128)} async-done(((f32[768,768]{1,0:T(8,128)}), f32[24,768]{1,0:T(8,128)}) %reduce-scatter.39.cloned.1.call-update) | async-done | bytes 73744
  1395.8 103.8 %reduce-scatter.43.cloned.1.call-done = f32[24,768]{1,0:T(8,128)} async-done(((f32[768,768]{1,0:T(8,128)}), f32[24,768]{1,0:T(8,128)}) %reduce-scatter.43.cloned.1.call-update) | async-done | bytes 73744
  1499.6 104.6 %reduce-scatter.41.cloned.1.call-done = f32[24,768]{1,0:T(8,128)} async-done(((f32[768,768]{1,0:T(8,128)}), f32[24,768]{1,0:T(8,128)}) %reduce-scatter.41.cloned.1.call-update) | async-done | bytes 73744
  1604.2 141.1 %reduce-scatter.27.cloned.1.call-done = f32[24,3072]{1,0:T(8,128)} async-done(((f32[768,3072]{1,0:T(8,128)}), f32[24,3072]{1,0:T(8,128)}) %reduce-scatter.27.cloned.1.call-update) | async-done | bytes 294928 | tf_op jit(solution)/shard_map/reduce_scatter | solution.py:487
  1745.3 142.0 %reduce-scatter.29.cloned.1.call-done = f32[96,768]{1,0:T(8,128)} async-done(((f32[3072,768]{1,0:T(8,128)}), f32[96,768]{1,0:T(8,128)}) %reduce-scatter.29.cloned.1.call-update) | async-done | bytes 294928 | tf_op jit(solution)/shard_map/reduce_scatter | solution.py:487
  (518 shorter events, 397.0 us)
Async XLA Ops:
  7.3 60.5 %all-gather.19.cloned.1.call-start = ((), (), s32[]{:S(2)}) async-start(), calls=%async_computation.13 | async-start | bytes 1216512 | tf_op jit(solution)/shard_map/all_gather | solution.py:324
  8.0 115.6 %all-gather.13.cloned.1.call-start = ((), (), s32[]{:S(2)}) async-start(), calls=%async_computation.10 | async-start | bytes 1216512 | tf_op jit(solution)/shard_map/all_gather | solution.py:325
  8.8 170.9 %all-gather.17.cloned.1.call-start = ((), (), s32[]{:S(2)}) async-start(), calls=%async_computation.12 | async-start | bytes 1216512 | tf_op jit(solution)/shard_map/all_gather | solution.py:322
  9.5 234.8 %all-gather.21.cloned.1.call-start = ((), (), s32[]{:S(2)}) async-start(), calls=%async_computation.14 | async-start | bytes 3932160 | tf_op jit(solution)/shard_map/all_gather | solution.py:252
  71.0 237.5 %all-gather.15.cloned.1.call-start = ((), (), s32[]{:S(2)}) async-start(), calls=%async_computation.11 | async-start | bytes 3932160 | tf_op jit(solution)/shard_map/all_gather | solution.py:253
  126.6 237.4 %all-gather.23.cloned.1.call-start = ((), (), s32[]{:S(2)}) async-start(), calls=%async_computation.15 | async-start | bytes 1216512 | tf_op jit(solution)/shard_map/all_gather | solution.py:327
  127.2 300.8 %all-gather.31.cloned.1.call-start = ((), (), s32[]{:S(2)}) async-start(), calls=%async_computation.19 | async-start | bytes 3932160 | tf_op jit(solution)/shard_map/all_gather | solution.py:252
  130.2 361.5 %all-gather.29.cloned.1.call-start = ((), (), s32[]{:S(2)}) async-start(), calls=%async_computation.18 | async-start | bytes 3932160 | tf_op jit(solution)/shard_map/all_gather | solution.py:253
  131.9 424.9 %all-gather.25.cloned.1.call-start = ((), (), s32[]{:S(2)}) async-start(), calls=%async_computation.16 | async-start | bytes 4866048 | tf_op jit(solution)/shard_map/all_gather | solution.py:331
  132.7 489.2 %all-gather.27.cloned.1.call-start = ((), (), s32[]{:S(2)}) async-start(), calls=%async_computation.17 | async-start | bytes 4866048 | tf_op jit(solution)/shard_map/all_gather | solution.py:333
  133.3 900.4 %reduce-scatter.37.cloned.1.call-start = ((), (), s32[]{:S(2)}) async-start(), calls=%async_computation.26 | async-start | bytes 3932160
  174.5 458.0 %copy-start.71 = (f32[768]{0:T(1024)}, f32[768]{0:T(1024)S(1)}, u32[]{:S(2)}) copy-start(f32[768]{0:T(1024)S(1)} %convert_element_type.274) | copy-start | bytes 9220
  174.5 458.0 %copy-start.73 = (f32[768]{0:T(1024)}, f32[768]{0:T(1024)S(1)}, u32[]{:S(2)}) copy-start(f32[768]{0:T(1024)S(1)} %convert_element_type.275) | copy-start | bytes 9220
  174.7 457.9 %copy-start.80 = (s32[4,128]{1,0:T(4,128)}, s32[4,128]{1,0:T(4,128)S(1)}, u32[]{:S(2)}) copy-start(s32[4,128]{1,0:T(4,128)S(1)} %get-tuple-element.166) | copy-start | bytes 6148
  503.5 415.8 %copy-start.8 = (f32[4,128,768]{2,1,0:T(8,128)}, f32[4,128,768]{2,1,0:T(8,128)S(1)}, u32[]{:S(2)}) copy-start(f32[4,128,768]{2,1,0:T(8,128)S(1)} %get-tuple-element.176) | copy-start | bytes 4718596
  937.5 123.2 %reduce-scatter.33.cloned.1.call-start = ((), (), s32[]{:S(2)}) async-start(), calls=%async_computation.24 | async-start | bytes 3932160
  955.7 167.6 %reduce-scatter.31.cloned.1.call-start = ((), (), s32[]{:S(2)}) async-start(), calls=%async_computation.23 | async-start | bytes 3932160
  983.5 202.8 %reduce-scatter.35.cloned.1.call-start = ((), (), s32[]{:S(2)}) async-start(), calls=%async_computation.25 | async-start | bytes 3932160
  1011.3 279.8 %reduce-scatter.25.cloned.1.call-start = ((), (), s32[]{:S(2)}) async-start(), calls=%async_computation.20 | async-start | bytes 2433024 | tf_op jit(solution)/shard_map/reduce_scatter | solution.py:487
  1017.2 378.6 %reduce-scatter.39.cloned.1.call-start = ((), (), s32[]{:S(2)}) async-start(), calls=%async_computation.27 | async-start | bytes 2433024
  1033.6 466.0 %reduce-scatter.43.cloned.1.call-start = ((), (), s32[]{:S(2)}) async-start(), calls=%async_computation.29 | async-start | bytes 2433024
  1071.5 532.7 %reduce-scatter.41.cloned.1.call-start = ((), (), s32[]{:S(2)}) async-start(), calls=%async_computation.28 | async-start | bytes 2433024
  1196.7 548.6 %reduce-scatter.27.cloned.1.call-start = ((), (), s32[]{:S(2)}) async-start(), calls=%async_computation.21 | async-start | bytes 9732096 | tf_op jit(solution)/shard_map/reduce_scatter | solution.py:487
  1207.6 679.7 %reduce-scatter.29.cloned.1.call-start = ((), (), s32[]{:S(2)}) async-start(), calls=%async_computation.22 | async-start | bytes 9732096 | tf_op jit(solution)/shard_map/reduce_scatter | solution.py:487
  (135 other events, 3304.3 us)
Sparse Core Ops, SparseCore 0:
  10.9 56.7 all-gather.18
  70.6 53.0 all-gather.12
  126.4 53.2 all-gather.16
  181.7 62.5 all-gather.20
  246.3 62.1 all-gather.14
  311.1 52.7 all-gather.22
  365.5 62.3 all-gather.30
  429.5 62.1 all-gather.28
  494.5 62.2 all-gather.24
  559.5 62.3 all-gather.26
  937.6 60.6 reduce-scatter.36
  1000.4 60.2 reduce-scatter.32
  1063.0 60.2 reduce-scatter.30
  1126.1 60.2 reduce-scatter.34
  1192.1 99.0 reduce-scatter.24
  1297.7 98.0 reduce-scatter.38
  1401.5 98.0 reduce-scatter.42
  1506.2 97.9 reduce-scatter.40
  1610.7 134.5 reduce-scatter.26
  1752.6 134.6 reduce-scatter.28
where the time goes:
time: 1900 us; the launch traced here: 1890 us
  waiting for transfers between devices  1150 us (61%)
  blocking collectives  337 us (18%)
  matrix products  215 us (11%)
  local copies, waits for them, and re-layouts  102 us (5%)
  other arithmetic  70.4 us (4%)
    unnamed x27, waiting for transfers between devices  453 us
    reduce_scatter x3, waiting for transfers between devices, per_device(): lax.psum_scatter(totals, ('blk', 'seq'), scatter_dimension=0, tiled=True)  291 us
    unnamed x5, blocking collectives  178 us
    all_gather x2, waiting for transfers between devices, keys_gathered(): lax.all_gather(keys_local, 'seq', axis=1, tiled=True)  118 us
    all_gather x2, waiting for transfers between devices, keys_gathered(): lax.all_gather(values_local, 'seq', axis=1, tiled=True)  103 us
    unnamed x332, local copies, waits for them, and re-layouts  80.9 us
    all_gather x1, blocking collectives, per_device(): lax.all_gather(document_vectors, ('blk', 'seq'), axis=0, tiled=True)  73.3 us
    all_gather x1, blocking collectives, per_device(): lax.all_gather(query_vectors, ('blk', 'seq'), axis=0, tiled=True)  71.8 us
  transfers between devices with their start and end apart: 20, of which 19 were waited for; matrix products, arithmetic and copies ran while one was open for 14% of the time, Pallas kernels for 0%

commit v1 on v0

v1 whole, which is shorter than its diff:
```python
import functools

import jax
import jax.numpy as jnp
from jax import lax
from jax.experimental import pallas as pl
from jax.experimental.pallas import tpu as pltpu
from jax.sharding import PartitionSpec as P

HEADS = 12
HEAD_DIM = 64
NQ = 2
SEGS = 4
TEMPERATURE = 0.05
NORM_EPSILON = 1e-06
MASKED = -1000000000.0
BF16 = jnp.bfloat16
F32 = jnp.float32
MESH = pl.DeviceIdType.MESH
ANY = pl.BlockSpec(memory_space=pl.ANY)
VMEM = pl.BlockSpec(memory_space=pltpu.VMEM)
SMEM = pl.BlockSpec(memory_space=pltpu.SMEM)
DMA = pltpu.SemaphoreType.DMA
VMEM_LIMIT = 60 * 2**20


def dot(a, b, ca=1, cb=0):
    return lax.dot_general(a, b, (((ca,), (cb,)), ((), ())), preferred_element_type=F32)


def struct(shape, dtype):
    return jax.ShapeDtypeStruct(shape, dtype)


def split_two(v):
    high = v.astype(BF16)
    return high, (v - high.astype(F32)).astype(BF16)


class Grid:
    def __init__(self, blk_size, seq_size):
        self.blk_size, self.seq_size = blk_size, seq_size
        self.kb = blk_size.bit_length() - 1
        self.ks = seq_size.bit_length() - 1
        assert 1 << self.kb == blk_size and 1 << self.ks == seq_size
        self.nd = self.kb + self.ks

    def here(self):
        return lax.axis_index("blk"), lax.axis_index("seq")

    def digit(self, b, q, d):
        if d < self.kb:
            w = 1 << (self.kb - 1 - d)
            return (b // w) % 2, w
        w = 1 << (self.nd - 1 - d)
        return (q // w) % 2, w

    def digits(self, b, q):
        return [self.digit(b, q, d)[0] for d in range(self.nd)]

    def partner(self, b, q, d):
        v, w = self.digit(b, q, d)
        if d < self.kb:
            return (b + (1 - 2 * v) * w, q)
        return (b, q + (1 - 2 * v) * w)

    def order(self, flavour):
        seq = list(range(self.kb, self.nd))
        head, last = list(range(self.kb))[:-1][::-1], [self.kb - 1]
        if head:
            r = flavour % len(head)
            head = head[r:] + head[:r]
        return seq + head + last

    def greet(self, b, q, partners, others):
        barrier = pltpu.get_barrier_semaphore()
        targets = [partners[d] for d in range(self.kb)]
        if others is None:
            targets += [partners[d] for d in range(self.kb, self.nd)]
        else:
            targets += [(b, o) for o in others]
        for t in targets:
            pl.semaphore_signal(barrier, inc=1, device_id=t, device_id_type=MESH)
        pl.semaphore_wait(barrier, len(targets))


def remote(src, dst, send, recv, where):
    return pltpu.make_async_remote_copy(
        src_ref=src, dst_ref=dst, send_sem=send, recv_sem=recv, device_id=where, device_id_type=MESH
    )


def flat_view(rows, lanes):
    if rows % 8 == 0:
        return rows, lanes
    return rows * lanes // 128, 128


def pieces(shapes):
    out = []
    for a, (rows, lanes) in enumerate(shapes):
        unit = 768 if rows < 64 else 256
        unit = min(unit, lanes)
        for lo in range(0, lanes, unit):
            half = unit // 2
            if half % 128 == 0:
                out.append([(a, lo, half, 0), (a, lo + half, half, 1)])
            else:
                out.append([(a, lo, unit, 0)])
    return out


def gather_kernel(grid, groups, n, lag, *refs):
    ins, tok = refs[:n], refs[n]
    outs, rows_out = refs[n + 1 : 2 * n + 1], refs[2 * n + 1]
    own_sem, send_sem, recv_sem, tok_own, tok_send, tok_recv = refs[2 * n + 2 :]
    b, q = grid.here()
    nd, ns = grid.nd, grid.seq_size
    my = grid.digits(b, q)
    partners = [grid.partner(b, q, d) for d in range(nd)]
    others = [lax.rem(q + j, ns) for j in range(1, ns)]
    grid.greet(b, q, partners, others)
    flat = [c for g in groups for c in g]
    where = {}
    first = 0
    for gi, g in enumerate(groups):
        where[gi] = list(range(first, first + len(g)))
        first += len(g)

    own = []
    for i, (a, lo, ln, _) in enumerate(flat):
        c = pltpu.make_async_copy(
            ins[a].at[:, pl.ds(lo, ln)],
            outs[a].at[tuple(my) + (slice(None), pl.ds(lo, ln))],
            own_sem.at[i],
        )
        c.start()
        own.append(c)
    copies = {}

    def stage(i, k):
        a, lo, ln, flavour = flat[i]
        order = grid.order(flavour)
        d = order[k]
        if k == 0:
            src = ins[a].at[:, pl.ds(lo, ln)]
            dst = outs[a].at[tuple(my) + (slice(None), pl.ds(lo, ln))]
        else:
            if k == 1:
                own[i].wait()
            copies[(i, k - 1)].wait_recv()
            done = order[:k]
            ix = tuple(slice(None) if e in done else my[e] for e in range(nd))
            ix = ix + (slice(None), pl.ds(lo, ln))
            src, dst = outs[a].at[ix], outs[a].at[ix]
        c = remote(src, dst, send_sem.at[i, k], recv_sem.at[i, k], partners[d])
        c.start()
        copies[(i, k)] = c

    row_copies = []
    total, lt, _ = tok.shape
    per = total // ns

    def send_rows():
        at = pl.ds(pl.multiple_of(q * lt, lt), lt)
        for r in range(per):
            c = pltpu.make_async_copy(tok.at[q * per + r], rows_out.at[r, at], tok_own.at[r])
            c.start()
            row_copies.append(c)
            for j in range(1, ns):
                o = others[j - 1]
                c = remote(
                    tok.at[o * per + r],
                    rows_out.at[r, at],
                    tok_send.at[j - 1, r],
                    tok_recv.at[j - 1, r],
                    (b, o),
                )
                c.start()
                row_copies.append(c)

    ng = len(groups)
    for t in range(ng + lag * (nd - 1)):
        for k in range(nd - 1, -1, -1):
            g = t - lag * k
            if 0 <= g < ng:
                for i in where[g]:
                    stage(i, k)
        if t == 2:
            send_rows()
    for i in range(len(flat)):
        copies[(i, nd - 1)].wait_recv()
    for i in range(len(flat)):
        for k in range(nd):
            copies[(i, k)].wait_send()
    for c in row_copies:
        c.wait()


def gather_all(grid, blocks, tokens, collective_id):
    nd, ns = grid.nd, grid.seq_size
    n = len(blocks)
    views = [x.reshape(flat_view(*x.shape)) for x in blocks]
    groups = pieces([v.shape for v in views])
    count = sum(len(g) for g in groups)
    total, lt, width = tokens.shape
    per = total // ns
    outs = [struct((2,) * nd + v.shape, v.dtype) for v in views]
    outs.append(struct((per, lt * ns, width), tokens.dtype))
    res = pl.pallas_call(
        functools.partial(gather_kernel, grid, groups, n, 2),
        out_shape=outs,
        in_specs=[VMEM] * (n + 1),
        out_specs=[ANY] * (n + 1),
        scratch_shapes=[
            DMA((count,)),
            DMA((count, nd)),
            DMA((count, nd)),
            DMA((per,)),
            DMA((ns - 1, per)),
            DMA((ns - 1, per)),
        ],
        compiler_params=pltpu.CompilerParams(
            collective_id=collective_id, has_side_effects=True, vmem_limit_bytes=VMEM_LIMIT
        ),
    )(*views, tokens)
    devices = 1 << nd
    full = [
        r.reshape((devices * x.shape[0], x.shape[1])) for r, x in zip(res[:-1], blocks, strict=True)
    ]
    return full, res[-1]


def reduce_plan(grid, flavour):
    free = list(range(grid.nd))
    plan = []
    for d in grid.order(flavour)[::-1]:
        pos = free.index(d)
        plan.append((d, 1 << pos, 1 << (len(free) - pos - 1)))
        free.remove(d)
    return plan


def scatter_kernel(grid, flat, n, nx, lag, *refs):
    nd, ns = grid.nd, grid.seq_size
    ins, rows_in = refs[:n], refs[n : n + nx]
    outs, rows_out = refs[n + nx : 2 * n + nx], refs[2 * n + nx : 2 * n + 2 * nx]
    rest = list(refs[2 * n + 2 * nx :])
    own_sem, send_sem, recv_sem, x_own, x_send, x_recv = rest[:6]
    bufs = rest[6:]
    b, q = grid.here()
    my = grid.digits(b, q)
    partners = [grid.partner(b, q, d) for d in range(nd)]
    others = [lax.rem(q + j, ns) for j in range(1, ns)]
    grid.greet(b, q, partners, others)

    row_copies = []
    for x in range(nx):
        per, length, _ = rows_in[x].shape
        lt = length // ns
        for r in range(per):
            at = pl.ds(pl.multiple_of(q * lt, lt), lt)
            c = pltpu.make_async_copy(
                rows_in[x].at[r, at], rows_out[x].at[q * per + r], x_own.at[x, r]
            )
            c.start()
            row_copies.append(c)

    def send_rows(x):
        per, length, _ = rows_in[x].shape
        lt = length // ns
        for r in range(per):
            for j in range(1, ns):
                o = others[j - 1]
                c = remote(
                    rows_in[x].at[r, pl.ds(pl.multiple_of(o * lt, lt), lt)],
                    rows_out[x].at[q * per + r],
                    x_send.at[x, j - 1, r],
                    x_recv.at[x, j - 1, r],
                    (b, o),
                )
                c.start()
                row_copies.append(c)

    per_piece = 1 + 2 * nd - 1
    copies, own = {}, {}

    def buffers(i):
        mine = bufs[i * per_piece : (i + 1) * per_piece]
        return mine[0], mine[1 : 1 + nd], mine[1 + nd :]

    for i, (a, lo, ln, flavour) in enumerate(flat):
        d = reduce_plan(grid, flavour)[0][0]
        ix = tuple(my[e] if e == d else slice(None) for e in range(nd)) + (slice(None), pl.ds(lo, ln))
        c = pltpu.make_async_copy(ins[a].at[ix], buffers(i)[0], own_sem.at[i])
        c.start()
        own[i] = c

    def send(i, k):
        a, lo, ln, flavour = flat[i]
        d, pre, post = reduce_plan(grid, flavour)[k]
        start, recv, acc = buffers(i)
        if k == 0:
            ix = tuple((1 - my[e]) if e == d else slice(None) for e in range(nd))
            src = ins[a].at[ix + (slice(None), pl.ds(lo, ln))]
        else:
            src = acc[k - 1].at[:, 1 - my[d]]
        c = remote(src, recv[k], send_sem.at[i, k], recv_sem.at[i, k], partners[d])
        c.start()
        copies[(i, k)] = c

    def add(i, k):
        a, lo, ln, flavour = flat[i]
        plan = reduce_plan(grid, flavour)
        d, pre, post = plan[k]
        start, recv, acc = buffers(i)
        copies[(i, k)].wait_recv()
        if k == 0:
            own[i].wait()
        if k == nd - 1:
            total = acc[k - 1][0, my[d], 0].astype(F32) + recv[k][0, 0].astype(F32)
            outs[a][:, lo : lo + ln] = total
            return
        _, pre2, post2 = plan[k + 1]

        def one(j, carry):
            if k == 0:
                ix = tuple((j // (1 << (nd - 2 - e))) % 2 for e in range(nd - 1))
                mine, other = start[ix], recv[0][ix]
            else:
                mine = acc[k - 1][j // post, my[d], j % post]
                other = recv[k][j // post, j % post]
            total = mine.astype(F32) + other.astype(F32)
            acc[k][j // (2 * post2), (j // post2) % 2, j % post2] = total.astype(acc[k].dtype)
            return carry

        lax.fori_loop(0, pre * post, one, 0)

    groups = sorted({c[4] for c in [(*f, gi) for f, gi in zip(flat, group_of(flat))]})
    members = {g: [i for i, gi in enumerate(group_of(flat)) if gi == g] for g in groups}
    ng = len(groups)
    for t in range(ng + lag * nd):
        for k in range(nd, -1, -1):
            g = t - lag * k
            if 0 <= g < ng:
                for i in members[g]:
                    if k > 0:
                        add(i, k - 1)
                    if k < nd:
                        send(i, k)
        if t == 0:
            for x in range(nx):
                send_rows(x)
    for i in range(len(flat)):
        for k in range(nd):
            copies[(i, k)].wait_send()
    for c in row_copies:
        c.wait()


def group_of(flat):
    ids, last = [], -1
    for _, _, _, flavour in flat:
        if flavour == 0:
            last += 1
        ids.append(last)
    return ids


def scatter_all(grid, grads, rows_back, collective_id):
    nd, ns = grid.nd, grid.seq_size
    devices = 1 << nd
    views, finals = [], []
    for g in grads:
        rows = g.shape[0] // devices
        finals.append((rows, g.shape[1]))
        views.append(g.reshape((2,) * nd + flat_view(rows, g.shape[1])))
    flat = [c for g in pieces([v.shape[-2:] for v in views]) for c in g]
    n, nx = len(views), len(rows_back)
    scratch = []
    for a, _, ln, flavour in flat:
        rows, dtype = views[a].shape[-2], views[a].dtype
        plan = reduce_plan(grid, flavour)
        scratch.append(pltpu.VMEM((2,) * (nd - 1) + (rows, ln), dtype))
        for k, (_, pre, post) in enumerate(plan):
            shape = (2,) * (nd - 1) if k == 0 else (pre, post)
            scratch.append(pltpu.VMEM(shape + (rows, ln), dtype))
        for _, pre, post in plan[1:]:
            scratch.append(pltpu.VMEM((pre, 2, post, rows, ln), dtype))
    outs = [struct(v.shape[-2:], F32) for v in views]
    for x in rows_back:
        per, length, width = x.shape
        outs.append(struct((per * ns, length // ns, width), x.dtype))
    per = rows_back[0].shape[0]
    count = len(flat)
    res = pl.pallas_call(
        functools.partial(scatter_kernel, grid, flat, n, nx, 2),
        out_shape=outs,
        in_specs=[ANY] * n + [ANY] * nx,
        out_specs=[VMEM] * n + [ANY] * nx,
        scratch_shapes=[
            DMA((count,)),
            DMA((count, nd)),
            DMA((count, nd)),
            DMA((nx, per)),
            DMA((nx, ns - 1, per)),
            DMA((nx, ns - 1, per)),
        ]
        + scratch,
        compiler_params=pltpu.CompilerParams(
            collective_id=collective_id, has_side_effects=True, vmem_limit_bytes=VMEM_LIMIT
        ),
    )(*views, *rows_back)
    return [r.reshape(s) for r, s in zip(res[:n], finals, strict=True)], res[n:]


def segment_of(lens, r, shape, axis, start=0):
    t = lax.broadcasted_iota(jnp.int32, shape, axis) + start
    end = lens[r, 0]
    seg = (t >= end).astype(jnp.int32)
    for k in range(1, SEGS):
        end = end + lens[r, k]
        seg = seg + (t >= end).astype(jnp.int32)
    return seg


def attention_kernel(
    lens, x_ref, wq, wk, wv, bq, bv, q_ref, k_ref, v_ref, p_ref, o_ref, vt_ref, ot_ref, bias_ref
):
    x = x_ref[0]
    length = x.shape[0]
    r = pl.program_id(0)
    seg_k = segment_of(lens, r, (length, 1), 0)
    seg_q = segment_of(lens, r, (1, length), 1)
    bias_ref[...] = jnp.where(seg_k == seg_q, 0.0, MASKED)
    q_ref[0] = ((dot(x, wq[...]) + bq[...]) * HEAD_DIM ** (-0.5)).astype(BF16)
    k_ref[0] = dot(x, wk[...]).astype(BF16)
    v = dot(x, wv[...]) + bv[...]
    v_ref[0] = v.astype(BF16)
    vt_ref[...] = v.T.astype(BF16)
    lane = lax.broadcasted_iota(jnp.int32, (1, 128), 1)

    def pair(p, carry):
        sl = pl.ds(pl.multiple_of(p * 128, 128), 128)
        qp, kp = q_ref[0, :, sl], k_ref[0, :, sl]
        for h in range(2):
            km = jnp.where(lane // HEAD_DIM == h, kp, jnp.zeros_like(kp))
            hs = pl.ds(pl.multiple_of(p * 128 + h * HEAD_DIM, HEAD_DIM), HEAD_DIM)
            s = dot(km, qp, 1, 1) + bias_ref[...]
            e = jnp.exp(s - jnp.max(s, axis=0, keepdims=True))
            pt = (e * (1.0 / jnp.sum(e, axis=0, keepdims=True))).astype(BF16)
            p_ref[0, p * 2 + h] = pt
            ot_ref[hs, :] = dot(vt_ref[hs, :], pt).astype(BF16)
        return carry

    lax.fori_loop(0, HEADS // 2, pair, 0)
    o_ref[0] = ot_ref[...].T


def attention(lens, x, wq, wk, wv, bq, bv):
    rows, length, width = x.shape
    row = lambda *s: pl.BlockSpec((1,) + s, lambda r: (r,) + (0,) * len(s))
    full = lambda *s: pl.BlockSpec(s, lambda r: (0,) * len(s))
    tokens = struct((rows, length, width), BF16)
    return pl.pallas_call(
        attention_kernel,
        grid=(rows,),
        out_shape=[tokens] * 3 + [struct((rows, HEADS, length, length), BF16), tokens],
        in_specs=[SMEM, row(length, width)] + [full(width, width)] * 3 + [full(1, width)] * 2,
        out_specs=[row(length, width)] * 3 + [row(HEADS, length, length), row(length, width)],
        scratch_shapes=[
            pltpu.VMEM((width, length), BF16),
            pltpu.VMEM((width, length), BF16),
            pltpu.VMEM((length, length), F32),
        ],
        compiler_params=pltpu.CompilerParams(vmem_limit_bytes=VMEM_LIMIT),
    )(lens, x, wq, wk, wv, bq, bv)


def layer_norm(v):
    c = v - jnp.mean(v, axis=-1, keepdims=True)
    inv = lax.rsqrt(jnp.mean(c * c, axis=-1, keepdims=True) + NORM_EPSILON)
    return c * inv, inv


def feed_kernel(
    tiles, lens, x_ref, o_ref, wo, bo, g1, s1, wi, bi, wd, bd, g2, s2,
    hid_ref, n1_ref, i1_ref, h1_ref, act_ref, slope_ref, n2_ref, i2_ref, pool_ref,
):
    t = pl.program_id(0)
    rows = x_ref.shape[0]
    pre1 = x_ref[...].astype(F32) + dot(o_ref[...], wo[...]) + bo[...]
    n1, i1 = layer_norm(pre1)
    h1 = n1 * g1[...] + s1[...]
    h1_low = h1.astype(BF16)
    n1_ref[...] = n1.astype(BF16)
    h1_ref[...] = h1_low
    i1_ref[...] = jnp.broadcast_to(i1, i1_ref.shape)
    acc = h1 + bd[...]
    chunk = wd.shape[1]
    for lo in range(0, wi.shape[1], chunk):
        sl = slice(lo, lo + chunk)
        inner = dot(h1_low, wi[:, sl]) + bi[:, sl]
        phi = 0.5 + 0.5 * lax.erf(inner * (0.5**0.5))
        act = (inner * phi).astype(BF16)
        act_ref[:, sl] = act
        density = jnp.exp(-0.5 * inner * inner) * 0.3989422804014327
        slope_ref[:, sl] = (phi + inner * density).astype(BF16)
        acc = acc + dot(act, wd[sl, :])
    n2, i2 = layer_norm(acc)
    h2 = n2 * g2[...] + s2[...]
    high, low = split_two(h2)
    hid_ref[...] = high
    n2_ref[...] = n2.astype(BF16)
    i2_ref[...] = jnp.broadcast_to(i2, i2_ref.shape)
    r = t // tiles
    seg = segment_of(lens, r, (1, rows), 1, (t % tiles) * rows)
    slot = jnp.where(seg < SEGS, r * SEGS + seg, -1)
    members = lax.broadcasted_iota(jnp.int32, (pool_ref.shape[0], rows), 0) == slot
    members = members.astype(F32).astype(BF16)
    part = dot(members, high) + dot(members, low)

    @pl.when(t == 0)
    def _():
        pool_ref[...] = part

    @pl.when(t != 0)
    def _():
        pool_ref[...] += part


def feed(lens, x, o, wo, bo, g1, s1, wi, bi, wd, bd, g2, s2, tile_rows):
    count, width = x.shape
    rows = lens.shape[0]
    ff = wi.shape[1]
    tiles = count // rows // tile_rows
    tile = lambda w: pl.BlockSpec((tile_rows, w), lambda t: (t, 0))
    full = lambda *s: pl.BlockSpec(s, lambda t: (0,) * len(s))
    vec = full(1, width)
    low, col = struct((count, width), BF16), struct((count, 128), F32)
    wide = struct((count, ff), BF16)
    return pl.pallas_call(
        functools.partial(feed_kernel, tiles),
        grid=(count // tile_rows,),
        out_shape=[low, low, col, low, wide, wide, low, col, struct((rows * SEGS, width), F32)],
        in_specs=[SMEM, tile(width), tile(width), full(width, width), vec, vec, vec]
        + [full(width, ff), full(1, ff), full(ff, width), vec, vec, vec],
        out_specs=[tile(width), tile(width), tile(128), tile(width), tile(ff), tile(ff)]
        + [tile(width), tile(128), full(rows * SEGS, width)],
        compiler_params=pltpu.CompilerParams(vmem_limit_bytes=VMEM_LIMIT),
    )(lens, x, o, wo, bo, g1, s1, wi, bi, wd, bd, g2, s2)


def contrast_kernel(grid, pool_ref, len_ref, pair_ref, pairs_ref, loss_ref, dpool_ref, emb, send_sem, recv_sem):
    nd = grid.nd
    b, q = grid.here()
    my = grid.digits(b, q)
    partners = [grid.partner(b, q, d) for d in range(nd)]
    own_rows, width = pool_ref.shape
    count = own_rows << nd
    avg = pool_ref[...] / len_ref[:, :1]
    inv = lax.rsqrt(jnp.sum(avg * avg, axis=-1, keepdims=True) + NORM_EPSILON)
    own = avg * inv
    emb[tuple(my)] = own
    grid.greet(b, q, partners, None)
    order = grid.order(0)
    for k, d in enumerate(order):
        ix = tuple(slice(None) if e in order[:k] else my[e] for e in range(nd))
        c = remote(emb.at[ix], emb.at[ix], send_sem.at[k], recv_sem.at[k], partners[d])
        c.start()
        c.wait()
    high, low = split_two(emb[...].reshape(count, width))
    own_high, own_low = split_two(own)
    scale = 1.0 / TEMPERATURE

    def product(ah, al, bh, bl, cb):
        return dot(ah, bh, 1, cb) + dot(ah, bl, 1, cb) + dot(al, bh, 1, cb)

    total = jnp.zeros((1, count), F32)
    step = min(count, 256)
    for lo in range(0, count, step):
        sim = product(high[lo : lo + step], low[lo : lo + step], high, low, 1) * scale
        at = lax.broadcasted_iota(jnp.int32, (step, 1), 0)
        total += jnp.sum(jnp.where(at % SEGS >= NQ, jnp.exp(sim - scale), 0.0), axis=0, keepdims=True)
    lse_cols = scale + jnp.log(total)
    sim = product(own_high, own_low, high, low, 1) * scale
    col = lax.broadcasted_iota(jnp.int32, (1, count), 1)
    row = lax.broadcasted_iota(jnp.int32, (own_rows, 1), 0) + (b * grid.seq_size + q) * own_rows
    col_doc, row_doc = col % SEGS >= NQ, row % SEGS >= NQ
    number = lambda at: (at // SEGS) * NQ + at % SEGS - NQ
    lse_rows = scale + jnp.log(
        jnp.sum(jnp.where(col_doc, jnp.exp(sim - scale), 0.0), axis=1, keepdims=True)
    )
    chosen = col_doc & (number(col) == pair_ref[:, :1])
    positive = jnp.sum(jnp.where(chosen, sim, 0.0), axis=1, keepdims=True)
    loss_ref[...] = jnp.broadcast_to(lse_rows - positive, loss_ref.shape)
    as_query = jnp.exp(sim - lse_rows) - chosen.astype(F32)
    chosen_by = number(row) == pairs_ref[:1]
    as_doc = jnp.exp(jnp.where(col_doc, MASKED, sim - lse_cols)) - chosen_by.astype(F32)
    grad = jnp.where(row_doc, jnp.where(col_doc, 0.0, as_doc), jnp.where(col_doc, as_query, 0.0))
    grad_high, grad_low = split_two(grad)
    demb = product(grad_high, grad_low, high, low, 0) * scale
    dpool = inv * demb - inv * inv * inv * avg * jnp.sum(avg * demb, axis=-1, keepdims=True)
    dpool_high, dpool_low = split_two(dpool / len_ref[:, :1])
    pad = jnp.zeros((64 - own_rows, width), F32)
    stacked = jnp.concatenate([dpool_high.astype(F32), pad, dpool_low.astype(F32), pad], axis=0)
    dpool_ref[...] = stacked.astype(BF16)


def contrast(grid, pool, len_col, pair_col, pair_row, collective_id):
    own_rows, width = pool.shape
    return pl.pallas_call(
        functools.partial(contrast_kernel, grid),
        out_shape=[struct((own_rows, 128), F32), struct((128, width), BF16)],
        in_specs=[VMEM] * 4,
        out_specs=[VMEM] * 2,
        scratch_shapes=[
            pltpu.VMEM((2,) * grid.nd + (own_rows, width), F32),
            DMA((grid.nd,)),
            DMA((grid.nd,)),
        ],
        compiler_params=pltpu.CompilerParams(
            collective_id=collective_id, has_side_effects=True, vmem_limit_bytes=VMEM_LIMIT
        ),
    )(pool, len_col, pair_col, pair_row)


def feed_back_kernel(
    tiles, lens, dp_ref, n2_ref, i2_ref, slope_ref, n1_ref, i1_ref, wd, wi, wo, g2, g1,
    dfeed_ref, dinner_ref, dbranch_ref, dpre1_ref, datt_ref, sums_ref, wide_ref,
):
    t = pl.program_id(0)
    rows = n2_ref.shape[0]

    @pl.when(t == 0)
    def _():
        sums_ref[...] = jnp.zeros_like(sums_ref)
        wide_ref[...] = jnp.zeros_like(wide_ref)

    def columns(v):
        return jnp.sum(v, axis=0, keepdims=True)

    def norm_back(g, n, inv):
        return inv * (
            g - jnp.mean(g, axis=-1, keepdims=True) - n * jnp.mean(g * n, axis=-1, keepdims=True)
        )

    r = t // tiles
    seg = segment_of(lens, r, (rows, 1), 0, (t % tiles) * rows)
    slot = jnp.where(seg < SEGS, r * SEGS + seg, -1)
    lane = lax.broadcasted_iota(jnp.int32, (rows, 128), 1)
    members = (lane % 64 == slot).astype(F32).astype(BF16)
    dh2 = dot(members, dp_ref[...])
    n2 = n2_ref[...].astype(F32)
    sums_ref[0:1] += columns(dh2 * n2)
    sums_ref[1:2] += columns(dh2)
    dpre2 = norm_back(dh2 * g2[...], n2, i2_ref[:, :1])
    dfeed = dpre2.astype(BF16)
    dfeed_ref[...] = dfeed
    sums_ref[2:3] += columns(dfeed.astype(F32))
    chunk = wd.shape[1]
    dh1 = dpre2
    for lo in range(0, wi.shape[1], chunk):
        sl = slice(lo, lo + chunk)
        dinner = (dot(dfeed, wd[sl, :], 1, 1) * slope_ref[:, sl].astype(F32)).astype(BF16)
        dinner_ref[:, sl] = dinner
        wide_ref[0:1, sl] += columns(dinner.astype(F32))
        dh1 = dh1 + dot(dinner, wi[:, sl], 1, 1)
    n1 = n1_ref[...].astype(F32)
    sums_ref[3:4] += columns(dh1 * n1)
    sums_ref[4:5] += columns(dh1)
    dpre1 = norm_back(dh1 * g1[...], n1, i1_ref[:, :1])
    dpre1_ref[...] = dpre1
    dbranch = dpre1.astype(BF16)
    dbranch_ref[...] = dbranch
    sums_ref[5:6] += columns(dbranch.astype(F32))
    datt_ref[...] = dot(dbranch, wo[...], 1, 1).astype(BF16)


def feed_back(lens, dp, n2, i2, slope, n1, i1, wd, wi, wo, g2, g1, tile_rows):
    count, width = n2.shape
    rows = lens.shape[0]
    ff = wi.shape[1]
    tiles = count // rows // tile_rows
    tile = lambda w: pl.BlockSpec((tile_rows, w), lambda t: (t, 0))
    full = lambda *s: pl.BlockSpec(s, lambda t: (0,) * len(s))
    low = struct((count, width), BF16)
    return pl.pallas_call(
        functools.partial(feed_back_kernel, tiles),
        grid=(count // tile_rows,),
        out_shape=[low, struct((count, ff), BF16), low, struct((count, width), F32), low]
        + [struct((8, width), F32), struct((8, ff), F32)],
        in_specs=[SMEM, full(128, width), tile(width), tile(128), tile(ff), tile(width), tile(128)]
        + [full(ff, width), full(width, ff), full(width, width), full(1, width), full(1, width)],
        out_specs=[tile(width), tile(ff), tile(width), tile(width), tile(width)]
        + [full(8, width), full(8, ff)],
        compiler_params=pltpu.CompilerParams(vmem_limit_bytes=VMEM_LIMIT),
    )(lens, dp, n2, i2, slope, n1, i1, wd, wi, wo, g2, g1)


def outer_kernel(a_ref, b_ref, o_ref):
    o_ref[...] = dot(a_ref[...], b_ref[...], 0, 0).astype(o_ref.dtype)


def outer(a, b, bm, bn):
    count, m = a.shape
    n = b.shape[1]
    return pl.pallas_call(
        outer_kernel,
        grid=(m // bm, n // bn),
        out_shape=struct((m, n), BF16),
        in_specs=[
            pl.BlockSpec((count, bm), lambda i, j: (0, i)),
            pl.BlockSpec((count, bn), lambda i, j: (0, j)),
        ],
        out_specs=pl.BlockSpec((bm, bn), lambda i, j: (i, j)),
        compiler_params=pltpu.CompilerParams(vmem_limit_bytes=VMEM_LIMIT),
    )(a, b)


def attention_back_kernel(q_ref, k_ref, v_ref, p_ref, do_ref, dq_ref, dk_ref, dv_ref, kt_ref, dqt_ref):
    kt_ref[...] = k_ref[0].T
    lane = lax.broadcasted_iota(jnp.int32, (1, 128), 1)

    def pair(p, carry):
        sl = pl.ds(pl.multiple_of(p * 128, 128), 128)
        qp, vp, dop = q_ref[0, :, sl], v_ref[0, :, sl], do_ref[0, :, sl]
        zero = jnp.zeros_like(vp)
        dv = dk = None
        for h in range(2):
            mine = lane // HEAD_DIM == h
            vm, dom, qm = (jnp.where(mine, u, zero) for u in (vp, dop, qp))
            hs = pl.ds(pl.multiple_of(p * 128 + h * HEAD_DIM, HEAD_DIM), HEAD_DIM)
            pt = p_ref[0, p * 2 + h]
            probs = pt.astype(F32)
            weighted = probs * dot(vm, dop, 1, 1)
            ds = (weighted - probs * jnp.sum(weighted, axis=0, keepdims=True)).astype(BF16)
            dv_h, dk_h = dot(pt, dom), dot(ds, qm)
            dv = dv_h if dv is None else dv + dv_h
            dk = dk_h if dk is None else dk + dk_h
            dqt_ref[hs, :] = (dot(kt_ref[hs, :], ds) * HEAD_DIM ** (-0.5)).astype(BF16)
        dv_ref[0, :, sl] = dv.astype(BF16)
        dk_ref[0, :, sl] = dk.astype(BF16)
        return carry

    lax.fori_loop(0, HEADS // 2, pair, 0)
    dq_ref[0] = dqt_ref[...].T


def attention_back(q, k, v, p, do):
    rows, length, width = q.shape
    row = lambda *s: pl.BlockSpec((1,) + s, lambda r: (r,) + (0,) * len(s))
    return pl.pallas_call(
        attention_back_kernel,
        grid=(rows,),
        out_shape=[struct((rows, length, width), BF16)] * 3,
        in_specs=[row(length, width)] * 3 + [row(HEADS, length, length), row(length, width)],
        out_specs=[row(length, width)] * 3,
        scratch_shapes=[pltpu.VMEM((width, length), BF16), pltpu.VMEM((width, length), BF16)],
        compiler_params=pltpu.CompilerParams(vmem_limit_bytes=VMEM_LIMIT),
    )(q, k, v, p, do)


def input_back_kernel(dpre1_ref, dq_ref, dk_ref, dv_ref, wq, wk, wv, out_ref, sums_ref):
    @pl.when(pl.program_id(0) == 0)
    def _():
        sums_ref[...] = jnp.zeros_like(sums_ref)

    sums_ref[0:1] += jnp.sum(dq_ref[...].astype(F32), axis=0, keepdims=True)
    sums_ref[1:2] += jnp.sum(dv_ref[...].astype(F32), axis=0, keepdims=True)
    total = dpre1_ref[...] + dot(dq_ref[...], wq[...], 1, 1)
    total += dot(dk_ref[...], wk[...], 1, 1) + dot(dv_ref[...], wv[...], 1, 1)
    out_ref[...] = total.astype(out_ref.dtype)


def input_back(dpre1, dq, dk, dv, wq, wk, wv, tile_rows):
    count, width = dpre1.shape
    tile = pl.BlockSpec((tile_rows, width), lambda t: (t, 0))
    full = lambda *s: pl.BlockSpec(s, lambda t: (0,) * len(s))
    return pl.pallas_call(
        input_back_kernel,
        grid=(count // tile_rows,),
        out_shape=[struct((count, width), BF16), struct((8, width), F32)],
        in_specs=[tile] * 4 + [full(width, width)] * 3,
        out_specs=[tile, full(8, width)],
        compiler_params=pltpu.CompilerParams(vmem_limit_bytes=VMEM_LIMIT),
    )(dpre1, dq, dk, dv, wq, wk, wv)


def pack_small(vectors, wide, extra):
    rows = [jnp.pad(v.astype(F32), (0, 128 - v.shape[0])) for v in (*vectors, wide, extra)]
    rows += [jnp.zeros((128,), F32)] * (16 - len(rows))
    return jnp.stack(rows)


def per_device(
    tokens, lengths, pair_ids, w_query, b_query, w_key, w_value, b_value, w_out, b_out,
    norm1_gain, norm1_bias, w_in, b_in, w_down, b_down, norm2_gain, norm2_bias,
):
    blk_size, seq_size = lax.axis_size("blk"), lax.axis_size("seq")
    grid = Grid(blk_size, seq_size)
    devices = blk_size * seq_size
    group_rows, local_len, width = tokens.shape
    rows = group_rows // seq_size
    length = local_len * seq_size
    count = rows * length
    ff = w_in.shape[1]
    part, wide_part, pairs = b_query.shape[0], b_in.shape[0], pair_ids.shape[0]

    lens = lax.dynamic_slice_in_dim(lengths, lax.axis_index("seq") * rows, rows, 0)
    vectors = (b_query, b_value, b_out, norm1_gain, norm1_bias, b_down, norm2_gain, norm2_bias)
    small = pack_small(vectors, b_in, pair_ids)
    full, x = gather_all(grid, (w_query, w_key, w_value, small, w_out, w_in, w_down), tokens, 1)
    wq, wk, wv, smalls, wo, wi, wd = full
    smalls = smalls.reshape(devices, 16, 128)
    vecs = smalls[:, : len(vectors), :part].transpose(1, 0, 2).reshape(len(vectors), 1, width)
    bq, bv, bo, g1, s1, bd, g2, s2 = (vecs[i] for i in range(len(vectors)))
    bi = smalls[:, len(vectors), :wide_part].reshape(1, ff)
    all_pairs = smalls[:, len(vectors) + 1, :pairs].reshape(-1, NQ).astype(jnp.int32)

    q, k, v, p, o = attention(lens, x, wq, wk, wv, bq, bv)
    x2, o2 = x.reshape(count, width), o.reshape(count, width)
    hid, n1, i1, h1, act, slope, n2, i2, pool = feed(
        lens, x2, o2, wo, bo, g1, s1, wi, bi, wd, bd, g2, s2, 256
    )

    none = jnp.full((all_pairs.shape[0], SEGS - NQ), -1, jnp.int32)
    pair_row = jnp.concatenate([all_pairs, none], axis=1).reshape(1, -1)
    own_pairs = jnp.concatenate([pair_ids.reshape(rows, NQ), none[:rows]], axis=1).reshape(-1, 1)
    pair_col = jnp.broadcast_to(own_pairs, (rows * SEGS, 128))
    len_col = jnp.broadcast_to(lens.reshape(-1, 1).astype(F32), (rows * SEGS, 128))
    losses, dpool = contrast(grid, pool, len_col, pair_col, pair_row, 2)
    query_loss = losses[:, 0].reshape(rows, SEGS)[:, :NQ].reshape(-1)

    dfeed, dinner, dbranch, dpre1, datt, sums, wide_sums = feed_back(
        lens, dpool, n2, i2, slope, n1, i1, wd, wi, wo, g2, g1, 256
    )
    grad_w_down = outer(act, dfeed, width, width)
    grad_w_in = outer(h1, dinner, width, width)
    grad_w_out = outer(o2, dbranch, width, width)
    dq, dk, dv = attention_back(q, k, v, p, datt.reshape(rows, length, width))
    dq, dk, dv = (d.reshape(count, width) for d in (dq, dk, dv))
    grad_x, sums_in = input_back(dpre1, dq, dk, dv, wq, wk, wv, 256)
    grad_w_query = outer(x2, dq, width, width)
    grad_w_key = outer(x2, dk, width, width)
    grad_w_value = outer(x2, dv, width, width)

    vec_grads = jnp.stack(
        [sums_in[0], sums_in[1], sums[5], sums[3], sums[4], sums[2], sums[0], sums[1]]
    )
    packed = jnp.pad(
        vec_grads.reshape(8, devices, part).transpose(1, 0, 2), ((0, 0), (0, 0), (0, 128 - part))
    )
    wide_grads = jnp.pad(
        wide_sums[0].reshape(devices, 1, wide_part), ((0, 0), (0, 7), (0, 128 - wide_part))
    )
    packed = jnp.concatenate([packed, wide_grads], axis=1).reshape(devices * 16, 128)
    grads, back = scatter_all(
        grid,
        (grad_w_down, grad_w_in, grad_w_out, packed, grad_w_query, grad_w_key, grad_w_value),
        (hid.reshape(rows, length, width), grad_x.reshape(rows, length, width)),
        3,
    )
    g_down, g_in, g_out, g_small, g_query, g_key, g_value = grads
    hidden_out, grad_tokens = back
    gv = [g_small[i, :part] for i in range(8)]
    return (
        hidden_out,
        query_loss,
        grad_tokens.astype(F32),
        g_query,
        gv[0],
        g_key,
        g_value,
        gv[1],
        g_out,
        gv[2],
        gv[3],
        gv[4],
        g_in,
        g_small[8, :wide_part],
        g_down,
        gv[5],
        gv[6],
        gv[7],
    )


def solution(mesh):
    both = ("blk", "seq")
    vec, mat, tok = P(both), P(both, None), P("blk", "seq", None)
    in_specs = (
        tok, P("blk", None), vec, mat, vec, mat, mat, vec, mat, vec, vec, vec, mat, vec, mat, vec,
        vec, vec,
    )
    out_specs = (
        tok, vec, tok, mat, vec, mat, mat, vec, mat, vec, vec, vec, mat, vec, mat, vec, vec, vec,
    )
    return jax.shard_map(
        per_device, mesh=mesh, in_specs=in_specs, out_specs=out_specs, check_vma=False
    )
```

time: 1900 us -> 414 us (0.22)
  waiting for transfers between devices: 1150 us -> 0 us
  Pallas kernels: 0 us -> 380 us
  blocking collectives: 337 us -> 0 us
  matrix products: 215 us -> 0 us
  local copies, waits for them, and re-layouts: 102 us -> 24.7 us
  other arithmetic: 70.4 us -> 7.52 us
    unnamed x27 -> x0, waiting for transfers between devices: 453 us -> none
    all_gather x10 -> x0, waiting for transfers between devices: 408 us -> none  [the longest x2 118 us: keys_gathered(): lax.all_gather(keys_local, 'seq', axis=1, tiled=True)]
    pallas_call x0 -> x14, Pallas kernels: none -> 380 us  [the longest x1 109 us: gather_all(): pl.pallas_call(functools.partial(gather_kernel, grid, groups, n, 2), out_...]
    reduce_scatter x3 -> x0, waiting for transfers between devices: 291 us -> none  [per_device(): lax.psum_scatter(totals, ('blk', 'seq'), scatter_dimension=0, tiled=True)]
    dot_general x56 -> x0, matrix products: 215 us -> none  [the longest x12 52.7 us: matmul_back(): jnp.einsum('rte,de->rtd', gradient, matrix, preferred_element_type=jnp.fl...]
    unnamed x5 -> x0, blocking collectives: 178 us -> none
    all_gather x3 -> x0, blocking collectives: 158 us -> none  [the longest x1 73.3 us: per_device(): lax.all_gather(document_vectors, ('blk', 'seq'), axis=0, tiled=True)]
    unnamed x332 -> x33, local copies, waits for them, and re-layouts: 80.9 us -> 5.28 us
  transfers between devices with their start and end apart: 20 -> 0, of which waited for: 19 -> 0; matrix products, arithmetic and copies ran while one was open for 14% -> 0% of each run, Pallas kernels for 0% -> 0%
where the time goes in v1:
time: 414 us; the launch traced here: 413 us
  Pallas kernels  380 us (92%)
  local copies, waits for them, and re-layouts  24.7 us (6%)
  other arithmetic  7.52 us (2%)
    pallas_call x1, Pallas kernels, gather_all(): pl.pallas_call(functools.partial(gather_kernel, grid, groups, n, 2), out_...  109 us
    pallas_call x1, Pallas kernels, scatter_all(): pl.pallas_call(functools.partial(scatter_kernel, grid, flat, n, nx, 2), o...  108 us
    pallas_call x6, Pallas kernels, outer(): pl.pallas_call(outer_kernel, grid=(m // bm, n // bn), out_shape=struct((m...  36 us
    pallas_call x1, Pallas kernels, attention(): pl.pallas_call(attention_kernel, grid=(rows,), out_shape=[tokens] * 3 + [...  26.5 us
    pallas_call x1, Pallas kernels, feed(): pl.pallas_call(functools.partial(feed_kernel, tiles), grid=(count // tile...  24.7 us
    pallas_call x1, Pallas kernels, attention_back(): pl.pallas_call(attention_back_kernel, grid=(rows,), out_shape=[struct((ro...  24.2 us
    pallas_call x1, Pallas kernels, feed_back(): pl.pallas_call(functools.partial(feed_back_kernel, tiles), grid=(count //...  22 us
    pallas_call x1, Pallas kernels, contrast(): pl.pallas_call(functools.partial(contrast_kernel, grid), out_shape=[struc...  21.3 us

profile of v1, /device:TPU:0, one launch (start us, length us, event | category | flops | bytes accessed | tf_op | source)
XLA Modules:
  0.0 413.1 jit_solution(7991268278339461646)
XLA Ops:
  5.8 1.2 stack.91.refs_3_
  8.3 109.2 %shard_map.313 = (bf16[2,2,2,2,2,24,768]{6,5,4,3,2,1,0:T(8,128)(2,1)}, bf16[2,2,2,2,2,24,768]{6,5,4,3,2,1,0:T(8,128)(2,1)}, bf16[2,2,2,2,2,24,768]{6,5,4,3,2,1,0...) custom-call(bf16[24,768]{1,0:T(8,128)(2,1)} %refs_0_.1, ...), custom_call_target="tpu_custom_call" | custom-call | tf_op jit(solution)/shard_map/pallas_call | solution.py:210
  117.5 0.9 slice.132
  119.1 0.9 slice.136
  120.0 0.9 slice.126
  127.2 26.5 %shard_map.314 = (bf16[2,512,768]{2,1,0:T(8,128)(2,1)}, bf16[2,512,768]{2,1,0:T(8,128)(2,1)}, bf16[2,512,768]{2,1,0:T(8,128)(2,1)}, bf16[2,12,512,512]{3,2,1,0:T(8,128)(2,1)}, bf16[2,512,768]{2,1,0:T(8,128)(2,1)}) custom-call(s32[2,4]{1,0:T(2,128)} %copy-done.9, bf16[2,512,768]{2,1,0:T(8,128)(2,1)} %get-tuple-element.63.x_ref, bf16[768,768]{1,0:T(8,128)(2,1)} %bitcast.104, ...), custom_call_target="tpu_custom_call" | custom-call | tf_op jit(solution)/shard_map/pallas_call | solution.py:465
  153.6 24.7 %shard_map.315 = (bf16[1024,768]{1,0:T(8,128)(2,1)}, bf16[1024,768]{1,0:T(8,128)(2,1)}, f32[1024,128]{1,0:T(8,128)}, bf16[1024,768]{1,0:T(8,128)(2,1)}, bf16[102...) custom-call(s32[2,4]{1,0:T(2,128)} %copy-done.9, ...), custom_call_target="tpu_custom_call" | custom-call | tf_op jit(solution)/shard_map/pallas_call | solution.py:542
  178.4 21.3 %shard_map.316 = (f32[8,128]{1,0:T(8,128)}, bf16[128,768]{1,0:T(8,128)(2,1)}) custom-call(f32[8,768]{1,0:T(8,128)} %get-tuple-element.73.pool_ref, f32[8,128]{1,0:T(8,128)} %broadcast_in_dim.6.len_ref, s32[8,128]{1,0:T(8,128)} %broadcast_in_dim.15.pair_ref, s32[1,256]{1,0:T(1,128)} %reshape.146.pairs_ref), custom_call_target="tpu_custom_call" | custom-call | tf_op jit(solution)/shard_map/pallas_call | solution.py:612
  199.7 22.0 %shard_map.317 = (bf16[1024,768]{1,0:T(8,128)(2,1)}, bf16[1024,3072]{1,0:T(8,128)(2,1)}, bf16[1024,768]{1,0:T(8,128)(2,1)}, f32[1024,768]{1,0:T(8,128)}, bf16[10...) custom-call(s32[2,4]{1,0:T(2,128)} %copy-done.9, bf16[128,768]{1,0:T(8,128)(2,1)} %get-tuple-element.74.dp_ref, ...), custom_call_target="tpu_custom_call" | custom-call | tf_op jit(solution)/shard_map/pallas_call | solution.py:688
  221.7 24.2 %shard_map.321 = (bf16[2,512,768]{2,1,0:T(8,128)(2,1)}, bf16[2,512,768]{2,1,0:T(8,128)(2,1)}, bf16[2,512,768]{2,1,0:T(8,128)(2,1)}) custom-call(bf16[2,512,768]{2,1,0:T(8,128)(2,1)} %get-tuple-element.85.q_ref, bf16[2,512,768]{2,1,0:T(8,128)(2,1)} %get-tuple-element.86.k_ref, bf16[2,512,768]{2,1,0:T(8,128)(2,1)} %get-tuple-element.87.v_ref, ...), custom_call_target="tpu_custom_call" | custom-call | tf_op jit(solution)/shard_map/pallas_call | solution.py:753
  245.9 8.7 %shard_map.322 = (bf16[1024,768]{1,0:T(8,128)(2,1)}, f32[8,768]{1,0:T(8,128)}) custom-call(f32[1024,768]{1,0:T(8,128)} %get-tuple-element.84.dpre1_ref, bf16[1024,768]{1,0:T(8,128)(2,1)} %bitcast.92, bf16[1024,768]{1,0:T(8,128)(2,1)} %bitcast.94, bf16[1024,768]{1,0:T(8,128)(2,1)} %bitcast.96, bf16[768,768]{1,0:T(8,128)(2,1)} %bitcast.105, ...), custom_call_target="tpu_custom_call" | custom-call | tf_op jit(solution)/shard_map/pallas_call | solution.py:780
  254.6 4.3 %shard_map.325 = bf16[768,768]{1,0:T(8,128)(2,1)} custom-call(bf16[1024,768]{1,0:T(8,128)(2,1)} %bitcast.81, bf16[1024,768]{1,0:T(8,128)(2,1)} %bitcast.97), custom_call_target="tpu_custom_call" | custom-call | tf_op jit(solution)/shard_map/pallas_call | solution.py:708
  258.9 4.3 %shard_map.324 = bf16[768,768]{1,0:T(8,128)(2,1)} custom-call(bf16[1024,768]{1,0:T(8,128)(2,1)} %bitcast.82, bf16[1024,768]{1,0:T(8,128)(2,1)} %bitcast.95), custom_call_target="tpu_custom_call" | custom-call | tf_op jit(solution)/shard_map/pallas_call | solution.py:708
  263.2 4.4 %shard_map.323 = bf16[768,768]{1,0:T(8,128)(2,1)} custom-call(bf16[1024,768]{1,0:T(8,128)(2,1)} %bitcast.83, bf16[1024,768]{1,0:T(8,128)(2,1)} %bitcast.93), custom_call_target="tpu_custom_call" | custom-call | tf_op jit(solution)/shard_map/pallas_call | solution.py:708
  268.3 4.3 %shard_map.320 = bf16[768,768]{1,0:T(8,128)(2,1)} custom-call(bf16[1024,768]{1,0:T(8,128)(2,1)} %bitcast.91, bf16[1024,768]{1,0:T(8,128)(2,1)} %get-tuple-element.83.b_ref), custom_call_target="tpu_custom_call" | custom-call | tf_op jit(solution)/shard_map/pallas_call | solution.py:708
  272.7 9.2 %shard_map.318 = bf16[3072,768]{1,0:T(8,128)(2,1)} custom-call(bf16[1024,3072]{1,0:T(8,128)(2,1)} %get-tuple-element.72.a_ref, bf16[1024,768]{1,0:T(8,128)(2,1)} %get-tuple-element.80.b_ref), custom_call_target="tpu_custom_call" | custom-call | tf_op jit(solution)/shard_map/pallas_call | solution.py:708
  282.7 0.9 slice_reduce_fusion
  283.9 0.9 copy.46
  284.7 9.5 %shard_map.319 = bf16[768,3072]{1,0:T(8,128)(2,1)} custom-call(bf16[1024,768]{1,0:T(8,128)(2,1)} %get-tuple-element.81.a_ref, bf16[1024,3072]{1,0:T(8,128)(2,1)} %get-tuple-element.82.b_ref), custom_call_target="tpu_custom_call" | custom-call | tf_op jit(solution)/shard_map/pallas_call | solution.py:708
  294.2 107.6 %shard_map.326 = (f32[96,768]{1,0:T(8,128)}, f32[24,3072]{1,0:T(8,128)}, f32[24,768]{1,0:T(8,128)}, f32[16,128]{1,0:T(8,128)}, f32[24,768]{1,0:T(8,128)}, /*inde...) custom-call(bf16[2,2,2,2,2,96,768]{6,5,4,3,2,1,0:T(8,128)(2,1)} %bitcast.88, ...), custom_call_target="tpu_custom_call" | custom-call | tf_op jit(solution)/shard_map/pallas_call | solution.py:396
  401.8 1.2 slice_bitcast_fusion.3
  402.9 1.5 slice_bitcast_fusion
  404.5 3.5 convert_element_type.54
  408.0 1.1 copy.60
  (73 shorter events, 19.1 us)
Async XLA Ops:
  0.7 4.9 %copy-start = (s32[8,4]{0,1:T(4,128)S(1)}, s32[8,4]{0,1:T(4,128)}, u32[]{:S(2)}) copy-start(s32[8,4]{0,1:T(4,128)} %param.19) | copy-start | bytes 388
  5.7 120.0 %copy-start.9 = (s32[2,4]{1,0:T(2,128)}, s32[2,4]{1,0:T(2,128)S(1)}, u32[]{:S(2)}) copy-start(s32[2,4]{1,0:T(2,128)S(1)} %copy.47.lens) | copy-start | bytes 100
  272.7 9.2 %copy-start.11 = (f32[8,128]{1,0:T(8,128)S(1)}, f32[8,128]{1,0:T(8,128)}, u32[]{:S(2)}) copy-start(f32[8,128]{1,0:T(8,128)} %get-tuple-element.99) | copy-start | bytes 12292
  272.7 10.0 %copy-start.10 = (f32[8,768]{1,0:T(8,128)S(1)}, f32[8,768]{1,0:T(8,128)}, u32[]{:S(2)}) copy-start(f32[8,768]{1,0:T(8,128)} %get-tuple-element.94) | copy-start | bytes 73732
  404.5 3.5 copy-start.2
  407.9 1.2 copy-start.8
  407.9 1.8 copy-start.7
  407.9 2.5 copy-start.6
  407.9 3.1 copy-start.5
  408.0 3.7 copy-start.4
  408.0 4.4 %copy-start.3 = (f32[96,768]{1,0:T(8,128)S(1)}, f32[96,768]{1,0:T(8,128)}, u32[]{:S(2)}) copy-start(f32[96,768]{1,0:T(8,128)} %get-tuple-element.168) | copy-start | bytes 884740
  408.0 5.1 %copy-start.1 = (s32[8,4]{0,1:T(4,128)S(1)}, s32[8,4]{0,1:T(4,128)}, u32[]{:S(2)}) copy-start(s32[8,4]{0,1:T(4,128)} %param.19) | copy-start | bytes 388

commit v2 on v1

--- a/solution.py
+++ b/solution.py
@@ -787,6 +787,431 @@
     )(dpre1, dq, dk, dv, wq, wk, wv)
 
 
+class Reducer:
+    def __init__(self, grid, flat, here, partners, my, sources, outs, own_sem, send_sem, recv_sem, bufs):
+        self.grid, self.flat, self.here, self.partners, self.my = grid, flat, here, partners, my
+        self.sources, self.outs = sources, outs
+        self.own_sem, self.send_sem, self.recv_sem = own_sem, send_sem, recv_sem
+        self.bufs = bufs
+        self.per_piece = 1 + grid.nd
+
+    def buf(self, i, k):
+        return self.bufs[i * self.per_piece + 1 + k]
+
+    def place(self, i, k):
+        order = self.grid.order(self.flat[i][3])[::-1]
+        free = [d for d in range(self.grid.nd) if d not in order[:k]]
+        return order[k], free.index(order[k])
+
+    def own(self, i):
+        a, lo, ln, _ = self.flat[i]
+        d, pos = self.place(i, 0)
+        ix = (slice(None),) * pos + (self.my[d],) + (slice(None),) * (self.grid.nd - pos - 1)
+        src = self.sources[a].at[ix + (slice(None), pl.ds(lo, ln))]
+        return pltpu.make_async_copy(src, self.bufs[i * self.per_piece], self.own_sem.at[i])
+
+    def copy(self, i, k):
+        a, lo, ln, _ = self.flat[i]
+        d, pos = self.place(i, k)
+        ix = (slice(None),) * pos + (1 - self.my[d],) + (slice(None),) * (self.grid.nd - k - pos - 1)
+        if k == 0:
+            src = self.sources[a].at[ix + (slice(None), pl.ds(lo, ln))]
+        else:
+            src = self.buf(i, k - 1).at[ix]
+        return remote(
+            src, self.buf(i, k), self.send_sem.at[i, k], self.recv_sem.at[i, k], self.partners[d]
+        )
+
+    def send(self, i, k):
+        if k == 0:
+            self.own(i).start()
+        self.copy(i, k).start()
+
+    def add(self, i, k):
+        nd = self.grid.nd
+        a, lo, ln, _ = self.flat[i]
+        d, pos = self.place(i, k)
+        self.copy(i, k).wait_recv()
+        if k == 0:
+            self.own(i).wait()
+        into = self.buf(i, k)
+        left = nd - k - 1
+        if left == 0:
+            total = self.buf(i, k - 1)[self.my[d]].astype(F32) + into[...].astype(F32)
+            self.outs[a][:, lo : lo + ln] = total
+            return
+
+        def one(j, carry):
+            ix = tuple((j // (1 << (left - 1 - e))) % 2 for e in range(left))
+            if k == 0:
+                mine = self.bufs[i * self.per_piece][ix]
+            else:
+                mine = self.buf(i, k - 1)[ix[:pos] + (self.my[d],) + ix[pos:]]
+            into[ix] = (mine.astype(F32) + into[ix].astype(F32)).astype(into.dtype)
+            return carry
+
+        lax.fori_loop(0, 1 << left, one, 0)
+
+    def step(self, i, k):
+        if k > 0:
+            self.add(i, k - 1)
+        if k < self.grid.nd:
+            self.send(i, k)
+
+    def finish(self):
+        for i in range(len(self.flat)):
+            for k in range(self.grid.nd):
+                self.copy(i, k).wait_send()
+
+
+def reducer_scratch(nd, flat, rows_of, dtype):
+    out = []
+    for a, _, ln, _ in flat:
+        out.append(pltpu.VMEM((2,) * (nd - 1) + (rows_of[a], ln), dtype))
+        for k in range(nd):
+            out.append(pltpu.VMEM((2,) * (nd - 1 - k) + (rows_of[a], ln), dtype))
+    return out
+
+
+SMALL_ROWS = 16
+ROW_BQ, ROW_BV, ROW_BO, ROW_G1, ROW_S1, ROW_BD, ROW_G2, ROW_S2, ROW_BI = range(9)
+
+
+def backward_kernel(grid, flat, n_bufs, tile_rows, *refs):
+    it = iter(refs)
+    take = lambda n: [next(it) for _ in range(n)]
+    lens, dp, g1, g2 = take(4)
+    n2, i2, slope, n1, i1, act, h1, o, q, k, v, p, x, hid = take(14)
+    w_down, w_in, w_out, w_query, w_key, w_value = take(6)
+    outs = take(6)
+    small_out, hid_back, gx_back = take(3)
+    dfeed, dinner, dbranch, dpre1, datt, dqkv, gx = take(7)
+    grads = take(6)
+    wd, wi, wo, wq, wk, wv = take(6)
+    small, small_recv = take(2)
+    own_sem, send_sem, recv_sem, ex_own, ex_send, ex_recv, w_sem, sm_send, sm_recv = take(9)
+    bufs = take(n_bufs)
+
+    b, sq = grid.here()
+    nd, ns = grid.nd, grid.seq_size
+    my = grid.digits(b, sq)
+    partners = [grid.partner(b, sq, d) for d in range(nd)]
+    others = [lax.rem(sq + j, ns) for j in range(1, ns)]
+    red = Reducer(grid, flat, (b, sq), partners, my, grads, outs, own_sem, send_sem, recv_sem, bufs)
+    rows, length, width = x.shape
+    count = rows * length
+    lt = length // ns
+    tiles = length // tile_rows
+
+    weight_loads = [
+        pltpu.make_async_copy(src, dst, w_sem.at[i])
+        for i, (src, dst) in enumerate(
+            [(w_down, wd), (w_in, wi), (w_out, wo), (w_query, wq), (w_key, wk), (w_value, wv)]
+        )
+    ]
+    for c in weight_loads:
+        c.start()
+    grid.greet(b, sq, partners, others)
+
+    def exchange(e, src, dst, r):
+        out = [
+            pltpu.make_async_copy(
+                src.at[r, pl.ds(pl.multiple_of(sq * lt, lt), lt)],
+                dst.at[sq * rows + r],
+                ex_own.at[e, r],
+            )
+        ]
+        for j in range(1, ns):
+            at = pl.ds(pl.multiple_of(others[j - 1] * lt, lt), lt)
+            out.append(
+                remote(
+                    src.at[r, at],
+                    dst.at[sq * rows + r],
+                    ex_send.at[e, r, j - 1],
+                    ex_recv.at[e, r, j - 1],
+                    (b, others[j - 1]),
+                )
+            )
+        return out
+
+    for r in range(rows):
+        for c in exchange(0, hid, hid_back, r):
+            c.start()
+    small[...] = jnp.zeros_like(small)
+
+    def columns(u):
+        return jnp.sum(u, axis=0, keepdims=True)
+
+    def norm_back(g, n, inv):
+        return inv * (
+            g - jnp.mean(g, axis=-1, keepdims=True) - n * jnp.mean(g * n, axis=-1, keepdims=True)
+        )
+
+    groups = []
+    for i, c in enumerate(flat):
+        if c[3] == 0:
+            groups.append([])
+        groups[-1].append(i)
+    early = len(groups) - 3
+
+    def slot(s):
+        for kk in range(nd, -1, -1):
+            g, odd = divmod(s - 2 * kk, 2)
+            if odd == 0 and 0 <= g < early:
+                for i in groups[g]:
+                    red.step(i, kk)
+
+    used = [0]
+
+    def hook(steps, active=True):
+        if not active:
+            return lambda: None
+        base = used[0]
+        used[0] += steps
+
+        def run():
+            now = pl.program_id(0)
+            for c in range(steps):
+                pl.when(now == c)(functools.partial(slot, base + c))
+
+        return run
+
+    weight_loads[0].wait()
+    weight_loads[1].wait()
+    weight_loads[2].wait()
+
+    def feed_body(n2_t, i2_t, slope_t, n1_t, i1_t, dfeed_t, dinner_t, dbranch_t, dpre1_t, datt_t):
+        t = pl.program_id(0)
+        r = t // tiles
+        seg = segment_of(lens, r, (tile_rows, 1), 0, (t % tiles) * tile_rows)
+        place = jnp.where(seg < SEGS, r * SEGS + seg, -1)
+        lane = lax.broadcasted_iota(jnp.int32, (tile_rows, 128), 1)
+        members = (lane % 64 == place).astype(F32).astype(BF16)
+        dh2 = dot(members, dp[...])
+        m2 = n2_t[...].astype(F32)
+        small[ROW_G2 : ROW_G2 + 1] += columns(dh2 * m2)
+        small[ROW_S2 : ROW_S2 + 1] += columns(dh2)
+        dpre2 = norm_back(dh2 * g2[...], m2, i2_t[:, :1])
+        low = dpre2.astype(BF16)
+        dfeed_t[...] = low
+        small[ROW_BD : ROW_BD + 1] += columns(low.astype(F32))
+        dh1 = dpre2
+        for c, lo in enumerate(range(0, wi.shape[1], width)):
+            sl = slice(lo, lo + width)
+            din = (dot(low, wd[sl, :], 1, 1) * slope_t[:, sl].astype(F32)).astype(BF16)
+            dinner_t[:, sl] = din
+            small[ROW_BI + c : ROW_BI + c + 1] += columns(din.astype(F32))
+            dh1 = dh1 + dot(din, wi[:, sl], 1, 1)
+        m1 = n1_t[...].astype(F32)
+        small[ROW_G1 : ROW_G1 + 1] += columns(dh1 * m1)
+        small[ROW_S1 : ROW_S1 + 1] += columns(dh1)
+        dp1 = norm_back(dh1 * g1[...], m1, i1_t[:, :1])
+        dpre1_t[...] = dp1
+        low = dp1.astype(BF16)
+        dbranch_t[...] = low
+        small[ROW_BO : ROW_BO + 1] += columns(low.astype(F32))
+        datt_t[0] = dot(low, wo[...], 1, 1).astype(BF16)
+
+    ff = wi.shape[1]
+    tile = lambda w: pl.BlockSpec((tile_rows, w), lambda t: (t, 0))
+    by_row = pl.BlockSpec((1, tile_rows, width), lambda t: (t // tiles, t % tiles, 0))
+    pltpu.emit_pipeline(
+        feed_body,
+        grid=(count // tile_rows,),
+        in_specs=[tile(width), tile(128), tile(ff), tile(width), tile(128)],
+        out_specs=[tile(width), tile(ff), tile(width), tile(width), by_row],
+    )(n2, i2, slope, n1, i1, dfeed, dinner, dbranch, dpre1, datt)
+
+    dev = (2,) * nd
+    zeros = (0,) * nd
+
+    def outer_call(a, g, dst, steps, a_map, g_map, block, out_map, active=True):
+        call_hook = hook(steps, active)
+
+        def body(a_t, g_t, out_t):
+            call_hook()
+            lhs = a_t[...].reshape(count, width)
+            rhs = g_t[...].reshape(count, width)
+            out_t[...] = dot(lhs, rhs, 0, 0).reshape(block).astype(BF16)
+
+        whole = lambda ref: (
+            (count, width) if len(ref.shape) == 2 else (1,) * (len(ref.shape) - 3) + (rows, length, width)
+        )
+        pltpu.emit_pipeline(
+            body,
+            grid=(steps,),
+            in_specs=[pl.BlockSpec(whole(a), a_map), pl.BlockSpec(whole(g), g_map)],
+            out_specs=[pl.BlockSpec(block, out_map)],
+        )(a, g, dst)
+
+    grad_in, grad_down, grad_out, grad_q, grad_k, grad_v = grads
+    square = dev + grad_out.shape[-2:]
+    at0 = lambda c: (0, 0)
+    chunks = ff // width
+    outer_call(
+        h1, dinner, grad_in, chunks, at0, lambda c: (0, c), square, lambda c: zeros + (0, c), False
+    )
+    down_rows = grad_down.shape[-2]
+    per = width // down_rows
+    low_digits = per.bit_length() - 1
+    top = nd - low_digits
+    outer_call(
+        act,
+        dfeed,
+        grad_down,
+        chunks,
+        lambda c: (0, c),
+        at0,
+        (1,) * top + (2,) * low_digits + (down_rows, width),
+        lambda c: tuple((c // (1 << (top - 1 - e))) % 2 for e in range(top)) + (0,) * low_digits + (0, 0),
+    )
+    outer_call(o, dbranch, grad_out, 1, at0, at0, square, lambda c: zeros + (0, 0))
+
+    for c in weight_loads[3:]:
+        c.wait()
+    lane = lax.broadcasted_iota(jnp.int32, (1, 128), 1)
+    for r in range(rows):
+        att_hook = hook(HEADS // 2)
+
+        def att_body(q_t, k_t, v_t, do_t, p_t, out_t):
+            att_hook()
+            qp, kp, vp, dop = q_t[0], k_t[0], v_t[0], do_t[0]
+            kt = kp.T
+            zero = jnp.zeros_like(vp)
+            dv = dk = None
+            dqt = []
+            for h in range(2):
+                mine = lane // HEAD_DIM == h
+                vm, dom, qm = (jnp.where(mine, u, zero) for u in (vp, dop, qp))
+                pt = p_t[0, h]
+                probs = pt.astype(F32)
+                weighted = probs * dot(vm, dop, 1, 1)
+                ds = (weighted - probs * jnp.sum(weighted, axis=0, keepdims=True)).astype(BF16)
+                dv_h, dk_h = dot(pt, dom), dot(ds, qm)
+                dv = dv_h if dv is None else dv + dv_h
+                dk = dk_h if dk is None else dk + dk_h
+                dqt.append(dot(kt[h * HEAD_DIM : (h + 1) * HEAD_DIM], ds) * HEAD_DIM ** (-0.5))
+            out_t[0, 0] = jnp.concatenate(dqt, axis=0).T.astype(BF16)
+            out_t[1, 0] = dk.astype(BF16)
+            out_t[2, 0] = dv.astype(BF16)
+
+        part = pl.BlockSpec((1, length, 128), lambda s, r=r: (r, 0, s))
+        pltpu.emit_pipeline(
+            att_body,
+            grid=(HEADS // 2,),
+            in_specs=[part] * 4 + [pl.BlockSpec((1, 2, length, length), lambda s, r=r: (r, s, 0, 0))],
+            out_specs=[pl.BlockSpec((3, 1, length, 128), lambda s, r=r: (0, r, 0, s))],
+        )(q, k, v, datt, p, dqkv)
+
+        in_hook = hook(tiles)
+
+        def in_body(dpre1_t, d_t, out_t):
+            in_hook()
+            dq, dk, dv = d_t[0, 0], d_t[1, 0], d_t[2, 0]
+            small[ROW_BQ : ROW_BQ + 1] += columns(dq.astype(F32))
+            small[ROW_BV : ROW_BV + 1] += columns(dv.astype(F32))
+            total = dpre1_t[...] + dot(dq, wq[...], 1, 1) + dot(dk, wk[...], 1, 1)
+            out_t[0] = (total + dot(dv, wv[...], 1, 1)).astype(BF16)
+
+        pltpu.emit_pipeline(
+            in_body,
+            grid=(tiles,),
+            in_specs=[
+                pl.BlockSpec((tile_rows, width), lambda t, r=r: (r * tiles + t, 0)),
+                pl.BlockSpec((3, 1, tile_rows, width), lambda t, r=r: (0, r, t, 0)),
+            ],
+            out_specs=[pl.BlockSpec((1, tile_rows, width), lambda t, r=r: (r, t, 0))],
+        )(dpre1, dqkv, gx)
+        for c in exchange(1, gx, gx_back, r):
+            c.start()
+
+    def small_copy(kk):
+        return remote(
+            small, small_recv.at[kk], sm_send.at[kk], sm_recv.at[kk], partners[order[kk]]
+        )
+
+    order = grid.order(0)[::-1]
+
+    def small_step(kk):
+        if kk > 0:
+            c = small_copy(kk - 1)
+            c.wait()
+            small[...] += small_recv[kk - 1]
+        if kk < nd:
+            small_copy(kk).start()
+
+    small_step(0)
+    for j, (d, dst) in enumerate(((0, grad_q), (1, grad_k), (2, grad_v))):
+        outer_call(
+            x, dqkv, dst, 1, lambda c: (0, 0, 0), lambda c, d=d: (d, 0, 0, 0), square,
+            lambda c: zeros + (0, 0),
+        )
+        if j > 0:
+            for i in groups[early + j - 1]:
+                red.step(i, 1)
+        small_step(j + 1)
+        for i in groups[early + j]:
+            red.step(i, 0)
+    s = used[0]
+    while s <= 2 * (early - 1) + 2 * nd:
+        slot(s)
+        s += 1
+    for t in range(2, 3 + nd):
+        for kk in range(nd, 0, -1):
+            g = t - kk
+            if 0 <= g < 3 and not (kk == 1 and g < 2):
+                for i in groups[early + g]:
+                    red.step(i, kk)
+        if 4 <= t + 1 <= nd:
+            small_step(t + 1)
+    small_out[...] = small[...]
+    red.finish()
+    for r in range(rows):
+        for e, (src, dst) in enumerate(((hid, hid_back), (gx, gx_back))):
+            for c in exchange(e, src, dst, r):
+                c.wait()
+
+
+def backward(grid, lens, dp, g1, g2, kept, weights, tile_rows, collective_id):
+    nd, ns = grid.nd, grid.seq_size
+    x, hid = kept[-2:]
+    rows, length, width = x.shape
+    count = rows * length
+    w_down, w_in = weights[0], weights[1]
+    ff = w_in.shape[1]
+    dev = (2,) * nd
+    part, down_part = width >> nd, ff >> nd
+    shapes = [(part, ff), (down_part, width)] + [(part, width)] * 4
+    flat = [c for g in pieces(shapes) for c in g]
+    rows_of = [s[0] for s in shapes]
+    bufs = reducer_scratch(nd, flat, rows_of, BF16)
+    back = struct((rows * ns, length // ns, width), BF16)
+    low = struct((count, width), BF16)
+    out_shape = [struct(s, F32) for s in shapes]
+    out_shape += [struct((SMALL_ROWS, width), F32), back, back]
+    out_shape += [low, struct((count, ff), BF16), low, struct((count, width), F32)]
+    out_shape += [struct((rows, length, width), BF16), struct((3, rows, length, width), BF16)]
+    out_shape += [struct((rows, length, width), BF16)]
+    out_shape += [struct(dev + s, BF16) for s in shapes]
+    n = len(flat)
+    res = pl.pallas_call(
+        functools.partial(backward_kernel, grid, flat, len(bufs), tile_rows),
+        out_shape=out_shape,
+        in_specs=[SMEM, VMEM, VMEM, VMEM] + [ANY] * (len(kept) + len(weights)),
+        out_specs=[VMEM] * 7 + [ANY] * (len(out_shape) - 7),
+        scratch_shapes=[pltpu.VMEM(w.shape, BF16) for w in weights]
+        + [pltpu.VMEM((SMALL_ROWS, width), F32), pltpu.VMEM((nd, SMALL_ROWS, width), F32)]
+        + [DMA((n,)), DMA((n, nd)), DMA((n, nd))]
+        + [DMA((2, rows)), DMA((2, rows, ns - 1)), DMA((2, rows, ns - 1))]
+        + [DMA((len(weights),)), DMA((nd,)), DMA((nd,))]
+        + bufs,
+        compiler_params=pltpu.CompilerParams(
+            collective_id=collective_id, has_side_effects=True, vmem_limit_bytes=VMEM_LIMIT
+        ),
+    )(lens, dp, g1, g2, *kept, *weights)
+    return res[:10]
+
+
 def pack_small(vectors, wide, extra):
     rows = [jnp.pad(v.astype(F32), (0, 128 - v.shape[0])) for v in (*vectors, wide, extra)]
     rows += [jnp.zeros((128,), F32)] * (16 - len(rows))
@@ -831,6 +1256,21 @@
     len_col = jnp.broadcast_to(lens.reshape(-1, 1).astype(F32), (rows * SEGS, 128))
     losses, dpool = contrast(grid, pool, len_col, pair_col, pair_row, 2)
     query_loss = losses[:, 0].reshape(rows, SEGS)[:, :NQ].reshape(-1)
+
+    if part % 8 == 0:
+        kept = (n2, i2, slope, n1, i1, act, h1, o2, q, k, v, p, x, hid.reshape(rows, length, width))
+        res = backward(grid, lens, dpool, g1, g2, kept, (wd, wi, wo, wq, wk, wv), 256, 3)
+        g_in, g_down, g_out, g_query, g_key, g_value, sums, hidden_out, grad_tokens = res[:9]
+        me = lax.axis_index("blk") * seq_size + lax.axis_index("seq")
+        own = lax.dynamic_slice_in_dim(sums[:8], me * part, part, 1)
+        gv = [own[i] for i in range(8)]
+        g_wide = lax.dynamic_slice_in_dim(
+            sums[ROW_BI : ROW_BI + ff // width].reshape(ff), me * wide_part, wide_part, 0
+        )
+        return (
+            hidden_out, query_loss, grad_tokens.astype(F32), g_query, gv[0], g_key, g_value, gv[1],
+            g_out, gv[2], gv[3], gv[4], g_in, g_wide, g_down, gv[5], gv[6], gv[7],
+        )
 
     dfeed, dinner, dbranch, dpre1, datt, sums, wide_sums = feed_back(
         lens, dpool, n2, i2, slope, n1, i1, wd, wi, wo, g2, g1, 256

time: 414 us -> 373 us (0.901)
  Pallas kernels: 380 us -> 342 us
    pallas_call x10 -> x1, Pallas kernels: 198 us -> 160 us  [backward(): pl.pallas_call(functools.partial(backward_kernel, grid, flat, len(bufs),...]
where the time goes in v2:
time: 373 us; the launch traced here: 372 us
  Pallas kernels  342 us (92%)
  local copies, waits for them, and re-layouts  21.8 us (6%)
  other arithmetic  7.49 us (2%)
    pallas_call x1, Pallas kernels, backward(): pl.pallas_call(functools.partial(backward_kernel, grid, flat, len(bufs),...  160 us
    pallas_call x1, Pallas kernels, gather_all(): pl.pallas_call(functools.partial(gather_kernel, grid, groups, n, 2), out_...  109 us
    pallas_call x1, Pallas kernels, attention(): pl.pallas_call(attention_kernel, grid=(rows,), out_shape=[tokens] * 3 + [...  26.4 us
    pallas_call x1, Pallas kernels, feed(): pl.pallas_call(functools.partial(feed_kernel, tiles), grid=(count // tile...  24.7 us
    pallas_call x1, Pallas kernels, contrast(): pl.pallas_call(functools.partial(contrast_kernel, grid), out_shape=[struc...  21.4 us

profile of v2, /device:TPU:0, one launch (start us, length us, event | category | flops | bytes accessed | tf_op | source)
XLA Modules:
  0.0 372.3 jit_solution(13311982410539071966)
XLA Ops:
  2.0 0.7 reshape.112
  2.8 0.7 bitcast_convert_fusion.6
  3.5 0.7 bitcast_convert_fusion.4
  4.2 0.7 bitcast_convert_fusion
  4.9 0.7 bitcast_convert_fusion.2
  5.8 1.2 stack.87.refs_3_
  8.3 109.2 %shard_map.313 = (bf16[2,2,2,2,2,24,768]{6,5,4,3,2,1,0:T(8,128)(2,1)}, bf16[2,2,2,2,2,24,768]{6,5,4,3,2,1,0:T(8,128)(2,1)}, bf16[2,2,2,2,2,24,768]{6,5,4,3,2,1,0...) custom-call(bf16[24,768]{1,0:T(8,128)(2,1)} %refs_0_.1, ...), custom_call_target="tpu_custom_call" | custom-call | tf_op jit(solution)/shard_map/pallas_call | solution.py:210
  117.5 0.9 slice.106
  118.4 0.7 reshape_squeeze.7.bi
  119.1 0.9 slice.110
  120.0 0.9 slice.100
  121.0 0.7 squeeze.55.s2
  122.4 0.7 squeeze.51.g1.refs_2_
  123.7 0.7 squeeze.52.s1
  127.1 26.4 %shard_map.314 = (bf16[2,512,768]{2,1,0:T(8,128)(2,1)}, bf16[2,512,768]{2,1,0:T(8,128)(2,1)}, bf16[2,512,768]{2,1,0:T(8,128)(2,1)}, bf16[2,12,512,512]{3,2,1,0:T(8,128)(2,1)}, bf16[2,512,768]{2,1,0:T(8,128)(2,1)}) custom-call(s32[2,4]{1,0:T(2,128)} %copy-done.9, bf16[2,512,768]{2,1,0:T(8,128)(2,1)} %get-tuple-element.51.x_ref.refs_16_, ...), custom_call_target="tpu_custom_call" | custom-call | tf_op jit(solution)/shard_map/pallas_call | solution.py:465
  153.5 24.7 %shard_map.315 = (bf16[1024,768]{1,0:T(8,128)(2,1)}, bf16[1024,768]{1,0:T(8,128)(2,1)}, f32[1024,128]{1,0:T(8,128)}, bf16[1024,768]{1,0:T(8,128)(2,1)}, bf16[102...) custom-call(s32[2,4]{1,0:T(2,128)} %copy-done.9, ...), custom_call_target="tpu_custom_call" | custom-call | tf_op jit(solution)/shard_map/pallas_call | solution.py:542
  178.3 21.4 %shard_map.316 = (f32[8,128]{1,0:T(8,128)}, bf16[128,768]{1,0:T(8,128)(2,1)}) custom-call(f32[8,768]{1,0:T(8,128)} %get-tuple-element.60.pool_ref, f32[8,128]{1,0:T(8,128)} %broadcast_in_dim.6.len_ref, s32[8,128]{1,0:T(8,128)} %broadcast_in_dim.15.pair_ref, s32[1,256]{1,0:T(1,128)} %reshape.113.pairs_ref), custom_call_target="tpu_custom_call" | custom-call | tf_op jit(solution)/shard_map/pallas_call | solution.py:612
  199.7 160.5 %shard_map.317 = (f32[24,3072]{1,0:T(8,128)}, f32[96,768]{1,0:T(8,128)}, f32[24,768]{1,0:T(8,128)}, f32[24,768]{1,0:T(8,128)}, f32[24,768]{1,0:T(8,128)}, /*inde...) custom-call(s32[2,4]{1,0:T(2,128)} %copy-done.9, ...), custom_call_target="tpu_custom_call" | custom-call | tf_op jit(solution)/shard_map/pallas_call | solution.py:1197
  360.9 0.7 slice.96
  361.7 0.7 slice.90
  363.6 3.5 convert_element_type.50
  367.1 1.1 copy.57
  370.8 0.7 copy.62
  371.6 0.7 copy.63
  (57 shorter events, 11.7 us)
Async XLA Ops:
  0.7 4.9 %copy-start = (s32[8,4]{0,1:T(4,128)S(1)}, s32[8,4]{0,1:T(4,128)}, u32[]{:S(2)}) copy-start(s32[8,4]{0,1:T(4,128)} %param.19) | copy-start | bytes 388
  5.7 120.0 %copy-start.9 = (s32[2,4]{1,0:T(2,128)}, s32[2,4]{1,0:T(2,128)S(1)}, u32[]{:S(2)}) copy-start(s32[2,4]{1,0:T(2,128)S(1)} %copy.44.lens.refs_0_) | copy-start | bytes 100
  199.7 160.5 %copy-start.10 = (f32[8,128]{1,0:T(8,128)S(1)}, f32[8,128]{1,0:T(8,128)}, u32[]{:S(2)}) copy-start(f32[8,128]{1,0:T(8,128)} %get-tuple-element.75) | copy-start | bytes 12292
  363.6 3.5 copy-start.2
  367.1 1.2 copy-start.8
  367.1 1.8 copy-start.7
  367.1 2.5 copy-start.6
  367.1 3.1 copy-start.5
  367.1 3.7 %copy-start.4 = (f32[24,3072]{1,0:T(8,128)S(1)}, f32[24,3072]{1,0:T(8,128)}, u32[]{:S(2)}) copy-start(f32[24,3072]{1,0:T(8,128)} %get-tuple-element.138) | copy-start | bytes 884740
  367.1 4.4 %copy-start.3 = (f32[96,768]{1,0:T(8,128)S(1)}, f32[96,768]{1,0:T(8,128)}, u32[]{:S(2)}) copy-start(f32[96,768]{1,0:T(8,128)} %get-tuple-element.140) | copy-start | bytes 884740
  367.1 5.1 %copy-start.1 = (s32[8,4]{0,1:T(4,128)S(1)}, s32[8,4]{0,1:T(4,128)}, u32[]{:S(2)}) copy-start(s32[8,4]{0,1:T(4,128)} %param.19) | copy-start | bytes 388

commit v3 on v2

--- a/solution.py
+++ b/solution.py
@@ -787,6 +787,350 @@
     )(dpre1, dq, dk, dv, wq, wk, wv)
 
 
+class Gatherer:
+    def __init__(self, grid, flat, partners, my, blocks, fulls, own_sem, send_sem, recv_sem):
+        self.grid, self.flat, self.partners, self.my = grid, flat, partners, my
+        self.blocks, self.fulls = blocks, fulls
+        self.own_sem, self.send_sem, self.recv_sem = own_sem, send_sem, recv_sem
+
+    def own(self, i):
+        a, lo, ln, _ = self.flat[i]
+        return pltpu.make_async_copy(
+            self.blocks[a].at[:, pl.ds(lo, ln)],
+            self.fulls[a].at[tuple(self.my) + (slice(None), pl.ds(lo, ln))],
+            self.own_sem.at[i],
+        )
+
+    def copy(self, i, k):
+        a, lo, ln, flavour = self.flat[i]
+        order = self.grid.order(flavour)
+        done = order[:k]
+        ix = tuple(slice(None) if e in done else self.my[e] for e in range(self.grid.nd))
+        dst = self.fulls[a].at[ix + (slice(None), pl.ds(lo, ln))]
+        src = self.blocks[a].at[:, pl.ds(lo, ln)] if k == 0 else dst
+        return remote(
+            src, dst, self.send_sem.at[i, k], self.recv_sem.at[i, k], self.partners[order[k]]
+        )
+
+    def step(self, i, k):
+        if k == 0:
+            self.own(i).start()
+        elif k == 1:
+            self.own(i).wait()
+        if k > 0:
+            self.copy(i, k - 1).wait_recv()
+        if k < self.grid.nd:
+            self.copy(i, k).start()
+
+    def finish(self):
+        for i in range(len(self.flat)):
+            for k in range(self.grid.nd):
+                self.copy(i, k).wait_send()
+
+
+def forward_kernel(grid, groups, tile_rows, *refs):
+    it = iter(refs)
+    take = lambda n: [next(it) for _ in range(n)]
+    lens, tok = take(2)
+    blocks = take(7)
+    spread, owner, spread_wide, owner_wide = take(4)
+    x_out, q_out, k_out, v_out, p_out, o_out = take(6)
+    n1_out, i1_out, h1_out, act_out, slope_out, n2_out, i2_out, hid_out = take(8)
+    full_out = take(7)
+    pool, vecs = take(2)
+    fulls = take(7)
+    x_s, q_s, k_s, v_s, vt_s, mask_s, h_s, bi_s = take(8)
+    own_sem, send_sem, recv_sem, tok_own, tok_send, tok_recv, out_sem = take(7)
+
+    b, sq = grid.here()
+    nd, ns = grid.nd, grid.seq_size
+    my = grid.digits(b, sq)
+    partners = [grid.partner(b, sq, d) for d in range(nd)]
+    others = [lax.rem(sq + j, ns) for j in range(1, ns)]
+    flat = [c for g in groups for c in g]
+    members, first = [], 0
+    for g in groups:
+        members.append(range(first, first + len(g)))
+        first += len(g)
+    ga = Gatherer(grid, flat, partners, my, blocks, fulls, own_sem, send_sem, recv_sem)
+    rows, length, width = x_s.shape
+    lt = length // ns
+    tiles = length // tile_rows
+    grid.greet(b, sq, partners, others)
+
+    def row_copy(r, j):
+        at = pl.ds(pl.multiple_of(sq * lt, lt), lt)
+        if j == 0:
+            return pltpu.make_async_copy(tok.at[sq * rows + r], x_s.at[r, at], tok_own.at[r])
+        o = others[j - 1]
+        return remote(
+            tok.at[o * rows + r], x_s.at[r, at], tok_send.at[r, j - 1], tok_recv.at[r, j - 1], (b, o)
+        )
+
+    plan = forward_plan(nd, len(groups), ns)
+
+    def run_at(point):
+        for g, k in plan.get(point, ()):
+            if k < 0:
+                row_copy(g, -k).start()
+            else:
+                for i in members[g]:
+                    ga.step(i, k)
+
+    def hook(name, steps):
+        def run():
+            now = pl.program_id(0)
+            for c in range(steps):
+                if (name, c) in plan:
+                    pl.when(now == c)(functools.partial(run_at, (name, c)))
+
+        return run
+
+    def arrived(*which):
+        for g in which:
+            for i in members[g]:
+                ga.step(i, nd)
+
+    out_copies = []
+
+    def put(src, dst):
+        c = pltpu.make_async_copy(src, dst, out_sem.at[len(out_copies)])
+        c.start()
+        out_copies.append(c)
+
+    for r in range(rows):
+        row_copy(r, 0).start()
+    run_at("start")
+    arrived(0, 1, 2)
+    part = blocks[1].shape[0]
+    smalls = fulls[0][...].reshape(1 << nd, 16, 128)
+    for i in range(8):
+        a = dot(smalls[:, i, :].astype(BF16), spread[...]) * owner[...]
+        vecs[i : i + 1] = jnp.sum(a, axis=0, keepdims=True)
+    a = dot(smalls[:, 8, :].astype(BF16), spread_wide[...]) * owner_wide[...]
+    bi_s[...] = jnp.sum(a, axis=0, keepdims=True)
+    bq, bv, bo, g1, s1, bd, g2, s2 = (vecs[i : i + 1] for i in range(8))
+    lane = lax.broadcasted_iota(jnp.int32, (1, 128), 1)
+
+    def square(ref):
+        return ref[...].reshape(width, width)
+
+    for r in range(rows):
+        run_at(("row", r))
+        for j in range(ns):
+            c = row_copy(r, j)
+            if j == 0:
+                c.wait()
+            else:
+                c.wait_recv()
+        put(x_s.at[r], x_out.at[r])
+        x = x_s[r]
+        q_s[r] = ((dot(x, square(fulls[1])) + bq) * HEAD_DIM ** (-0.5)).astype(BF16)
+        k_s[r] = dot(x, square(fulls[2])).astype(BF16)
+        v = dot(x, square(fulls[3])) + bv
+        v_s[r] = v.astype(BF16)
+        vt_s[...] = v.T.astype(BF16)
+        for src, dst in ((q_s, q_out), (k_s, k_out), (v_s, v_out)):
+            put(src.at[r], dst.at[r])
+        seg_k = segment_of(lens, r, (length, 1), 0)
+        seg_q = segment_of(lens, r, (1, length), 1)
+        mask_s[...] = jnp.where(seg_k == seg_q, 0.0, MASKED)
+        att_hook = hook(("attention", r), HEADS // 2)
+
+        def att_body(p_t, o_t, r=r):
+            att_hook()
+            p = pl.program_id(0)
+            sl = pl.ds(pl.multiple_of(p * 128, 128), 128)
+            qp, kp = q_s[r, :, sl], k_s[r, :, sl]
+            out = []
+            for h in range(2):
+                km = jnp.where(lane // HEAD_DIM == h, kp, jnp.zeros_like(kp))
+                hs = pl.ds(pl.multiple_of(p * 128 + h * HEAD_DIM, HEAD_DIM), HEAD_DIM)
+                s = dot(km, qp, 1, 1) + mask_s[...]
+                e = jnp.exp(s - jnp.max(s, axis=0, keepdims=True))
+                pt = (e * (1.0 / jnp.sum(e, axis=0, keepdims=True))).astype(BF16)
+                p_t[0, h] = pt
+                out.append(dot(vt_s[hs, :], pt))
+            o_t[0] = jnp.concatenate(out, axis=0).T.astype(BF16)
+
+        pltpu.emit_pipeline(
+            att_body,
+            grid=(HEADS // 2,),
+            out_specs=[
+                pl.BlockSpec((1, 2, length, length), lambda s, r=r: (r, s, 0, 0)),
+                pl.BlockSpec((1, length, 128), lambda s, r=r: (r, 0, s)),
+            ],
+        )(p_out, o_out)
+
+    run_at("in")
+    down_groups = width // 256
+    arrived(*range(3, len(groups) - down_groups))
+    for a in range(6):
+        put(fulls[a], full_out[a])
+    ff = bi_s.shape[1]
+    tile = lambda w: pl.BlockSpec((tile_rows, w), lambda t: (t, 0))
+
+    def tile_at():
+        t = pl.program_id(0)
+        start = lax.rem(t, tiles) * tile_rows
+        return t // tiles, start, pl.ds(pl.multiple_of(start, tile_rows), tile_rows)
+
+    in_hook = hook("in", rows * tiles)
+
+    def in_body(o_t, n1_t, i1_t, h1_t, act_t, slope_t):
+        in_hook()
+        r, _, at = tile_at()
+        pre1 = x_s[r, at].astype(F32) + dot(o_t[0], square(fulls[4])) + bo
+        n1, i1 = layer_norm(pre1)
+        h1 = n1 * g1 + s1
+        low = h1.astype(BF16)
+        h_s[r, at] = h1
+        n1_t[...] = n1.astype(BF16)
+        i1_t[...] = jnp.broadcast_to(i1, i1_t.shape)
+        h1_t[...] = low
+        for lo in range(0, ff, width):
+            w = fulls[5][(slice(None),) * (nd + 1) + (slice(lo, lo + width),)]
+            inner = dot(low, w.reshape(width, width)) + bi_s[:, lo : lo + width]
+            phi = 0.5 + 0.5 * lax.erf(inner * (0.5**0.5))
+            act_t[:, lo : lo + width] = (inner * phi).astype(BF16)
+            density = jnp.exp(-0.5 * inner * inner) * 0.3989422804014327
+            slope_t[:, lo : lo + width] = (phi + inner * density).astype(BF16)
+
+    pltpu.emit_pipeline(
+        in_body,
+        grid=(rows * tiles,),
+        in_specs=[pl.BlockSpec((1, tile_rows, width), lambda t: (t // tiles, t % tiles, 0))],
+        out_specs=[tile(width), tile(128), tile(width), tile(ff), tile(ff)],
+    )(o_out, n1_out, i1_out, h1_out, act_out, slope_out)
+
+    run_at("down")
+    arrived(*range(len(groups) - down_groups, len(groups)))
+    put(fulls[6], full_out[6])
+    pool[...] = jnp.zeros_like(pool)
+    down_rows = blocks[6].shape[0]
+    top = nd - ((width // down_rows).bit_length() - 1)
+
+    def down_body(act_t, hid_t, n2_t, i2_t):
+        r, start, at = tile_at()
+        acc = h_s[r, at] + bd
+        for c, lo in enumerate(range(0, ff, width)):
+            ix = tuple((c >> (top - 1 - e)) % 2 for e in range(top))
+            acc = acc + dot(act_t[:, lo : lo + width], fulls[6][ix].reshape(width, width))
+        n2, i2 = layer_norm(acc)
+        high, low = split_two(n2 * g2 + s2)
+        hid_t[...] = high
+        n2_t[...] = n2.astype(BF16)
+        i2_t[...] = jnp.broadcast_to(i2, i2_t.shape)
+        seg = segment_of(lens, r, (1, tile_rows), 1, start)
+        slot = jnp.where(seg < SEGS, r * SEGS + seg, -1)
+        mine = lax.broadcasted_iota(jnp.int32, (pool.shape[0], tile_rows), 0) == slot
+        mine = mine.astype(F32).astype(BF16)
+        pool[...] += dot(mine, high) + dot(mine, low)
+
+    pltpu.emit_pipeline(
+        down_body,
+        grid=(rows * tiles,),
+        in_specs=[tile(ff)],
+        out_specs=[tile(width), tile(width), tile(128)],
+    )(act_out, hid_out, n2_out, i2_out)
+
+    ga.finish()
+    for r in range(rows):
+        for j in range(1, ns):
+            row_copy(r, j).wait_send()
+    for c in out_copies:
+        c.wait()
+
+
+FORWARD_PLAN = {
+    "start": (
+        (1, 0), (2, 0), (0, 0), (6, 0), (1, 1), (5, 0), (4, 0), (0, 1), (2, 1), (8, 0),
+        (1, 2), (7, 0), (0, 2), (2, 2), (3, 0), (1, 3), (4, 1), (5, 1), (8, 1), (0, 3),
+        (0, -2), (4, 2), (1, 4), (3, 1), (7, 1), (6, 1), (0, -3), (0, -1), (2, 3), (0, 4),
+        (8, 2), (1, -1), (1, -3), (5, 2), (3, 2), (1, -2), (2, 4), (7, 2), (6, 2), (5, 3),
+        (8, 3), (3, 3), (9, 0), (10, 0), (4, 3), (7, 3),
+    ),
+    (("attention", 0), 3): (
+        (8, 4),
+    ),
+    ("row", 1): (
+        (5, 4), (4, 4), (3, 4), (6, 3),
+    ),
+    (("attention", 1), 0): (
+        (10, 1),
+    ),
+    (("attention", 1), 1): (
+        (9, 1),
+    ),
+    (("attention", 1), 2): (
+        (7, 4), (10, 2), (6, 4),
+    ),
+    (("attention", 1), 4): (
+        (9, 2),
+    ),
+    (("attention", 1), 5): (
+        (10, 3),
+    ),
+    ("in", 3): (
+        (10, 4), (9, 4),
+    ),
+    "in": (
+        (9, 3),
+    ),
+}
+def forward_plan(nd, groups, ns):
+    if nd == 5 and groups == 11 and ns == 4:
+        return FORWARD_PLAN
+    ops = []
+    for t in range(groups + 2 * nd):
+        ops += [(t - 2 * k, k) for k in range(nd - 1, -1, -1) if 0 <= t - 2 * k < groups]
+        if t == nd:
+            ops += [(r, -j) for r in range(2) for j in range(1, ns)]
+    return {"start": tuple(ops)}
+
+
+def forward(grid, lens, tokens, blocks, tile_rows, collective_id):
+    nd, ns = grid.nd, grid.seq_size
+    total, lt, width = tokens.shape
+    rows, length = total // ns, lt * ns
+    count = rows * length
+    ff = blocks[5].shape[1]
+    part, wide_part = width >> nd, ff >> nd
+    dev = (2,) * nd
+    groups = pieces([x.shape for x in blocks])
+    groups = [groups[0] + groups[1]] + groups[2:]
+    n = sum(len(g) for g in groups)
+    lane, col = jnp.arange(128)[:, None], jnp.arange(width)[None, :]
+    spread = (lane == col % part).astype(BF16)
+    owner = (jnp.arange(1 << nd)[:, None] == col // part).astype(F32)
+    col = jnp.arange(ff)[None, :]
+    spread_wide = (lane == col % wide_part).astype(BF16)
+    owner_wide = (jnp.arange(1 << nd)[:, None] == col // wide_part).astype(F32)
+    seq3 = struct((rows, length, width), BF16)
+    low, stat = struct((count, width), BF16), struct((count, 128), F32)
+    wide = struct((count, ff), BF16)
+    out_shape = [seq3] * 4 + [struct((rows, HEADS, length, length), BF16), seq3]
+    out_shape += [low, stat, low, wide, wide, low, stat, low]
+    out_shape += [struct(dev + x.shape, x.dtype) for x in blocks]
+    out_shape += [struct((rows * SEGS, width), F32), struct((8, width), F32)]
+    res = pl.pallas_call(
+        functools.partial(forward_kernel, grid, groups, tile_rows),
+        out_shape=out_shape,
+        in_specs=[SMEM] + [VMEM] * 12,
+        out_specs=[ANY] * (len(out_shape) - 2) + [VMEM] * 2,
+        scratch_shapes=[pltpu.VMEM(dev + x.shape, x.dtype) for x in blocks]
+        + [pltpu.VMEM((rows, length, width), BF16)] * 4
+        + [pltpu.VMEM((width, length), BF16), pltpu.VMEM((length, length), F32)]
+        + [pltpu.VMEM((rows, length, width), F32), pltpu.VMEM((1, ff), F32)]
+        + [DMA((n,)), DMA((n, nd)), DMA((n, nd))]
+        + [DMA((rows,)), DMA((rows, ns - 1)), DMA((rows, ns - 1)), DMA((7 + 4 * rows,))],
+        compiler_params=pltpu.CompilerParams(
+            collective_id=collective_id, has_side_effects=True, vmem_limit_bytes=VMEM_LIMIT
+        ),
+    )(lens, tokens, *blocks, spread, owner, spread_wide, owner_wide)
+    return res
+
+
 class Reducer:
     def __init__(self, grid, flat, here, partners, my, sources, outs, own_sem, send_sem, recv_sem, bufs):
         self.grid, self.flat, self.here, self.partners, self.my = grid, flat, here, partners, my
@@ -1065,7 +1409,7 @@
         (1,) * top + (2,) * low_digits + (down_rows, width),
         lambda c: tuple((c // (1 << (top - 1 - e))) % 2 for e in range(top)) + (0,) * low_digits + (0, 0),
     )
-    outer_call(o, dbranch, grad_out, 1, at0, at0, square, lambda c: zeros + (0, 0))
+    outer_call(o, dbranch, grad_out, 1, lambda c: (0, 0, 0), at0, square, lambda c: zeros + (0, 0))
 
     for c in weight_loads[3:]:
         c.wait()
@@ -1235,19 +1579,32 @@
     lens = lax.dynamic_slice_in_dim(lengths, lax.axis_index("seq") * rows, rows, 0)
     vectors = (b_query, b_value, b_out, norm1_gain, norm1_bias, b_down, norm2_gain, norm2_bias)
     small = pack_small(vectors, b_in, pair_ids)
-    full, x = gather_all(grid, (w_query, w_key, w_value, small, w_out, w_in, w_down), tokens, 1)
-    wq, wk, wv, smalls, wo, wi, wd = full
-    smalls = smalls.reshape(devices, 16, 128)
-    vecs = smalls[:, : len(vectors), :part].transpose(1, 0, 2).reshape(len(vectors), 1, width)
-    bq, bv, bo, g1, s1, bd, g2, s2 = (vecs[i] for i in range(len(vectors)))
-    bi = smalls[:, len(vectors), :wide_part].reshape(1, ff)
+    fused = part % 8 == 0
+    if fused:
+        res = forward(
+            grid, lens, tokens, (small, w_query, w_key, w_value, w_out, w_in, w_down), 256, 4
+        )
+        x, q, k, v, p, o, n1, i1, h1, act, slope, n2, i2, hid = res[:14]
+        smalls = res[14].reshape(devices, 16, 128)
+        wq, wk, wv, wo, wi, wd = (
+            w.reshape((devices * w.shape[-2], w.shape[-1])) for w in res[15:21]
+        )
+        pool, vecs = res[21:]
+        g1, g2 = vecs[3:4], vecs[6:7]
+    else:
+        full, x = gather_all(grid, (w_query, w_key, w_value, small, w_out, w_in, w_down), tokens, 1)
+        wq, wk, wv, smalls, wo, wi, wd = full
+        smalls = smalls.reshape(devices, 16, 128)
+        vecs = smalls[:, : len(vectors), :part].transpose(1, 0, 2).reshape(len(vectors), 1, width)
+        bq, bv, bo, g1, s1, bd, g2, s2 = (vecs[i] for i in range(len(vectors)))
+        bi = smalls[:, len(vectors), :wide_part].reshape(1, ff)
+
+        q, k, v, p, o = attention(lens, x, wq, wk, wv, bq, bv)
+        x2, o2 = x.reshape(count, width), o.reshape(count, width)
+        hid, n1, i1, h1, act, slope, n2, i2, pool = feed(
+            lens, x2, o2, wo, bo, g1, s1, wi, bi, wd, bd, g2, s2, 256
+        )
     all_pairs = smalls[:, len(vectors) + 1, :pairs].reshape(-1, NQ).astype(jnp.int32)
-
-    q, k, v, p, o = attention(lens, x, wq, wk, wv, bq, bv)
-    x2, o2 = x.reshape(count, width), o.reshape(count, width)
-    hid, n1, i1, h1, act, slope, n2, i2, pool = feed(
-        lens, x2, o2, wo, bo, g1, s1, wi, bi, wd, bd, g2, s2, 256
-    )
 
     none = jnp.full((all_pairs.shape[0], SEGS - NQ), -1, jnp.int32)
     pair_row = jnp.concatenate([all_pairs, none], axis=1).reshape(1, -1)
@@ -1257,8 +1614,8 @@
     losses, dpool = contrast(grid, pool, len_col, pair_col, pair_row, 2)
     query_loss = losses[:, 0].reshape(rows, SEGS)[:, :NQ].reshape(-1)
 
-    if part % 8 == 0:
-        kept = (n2, i2, slope, n1, i1, act, h1, o2, q, k, v, p, x, hid.reshape(rows, length, width))
+    if fused:
+        kept = (n2, i2, slope, n1, i1, act, h1, o, q, k, v, p, x, hid.reshape(rows, length, width))
         res = backward(grid, lens, dpool, g1, g2, kept, (wd, wi, wo, wq, wk, wv), 256, 3)
         g_in, g_down, g_out, g_query, g_key, g_value, sums, hidden_out, grad_tokens = res[:9]
         me = lax.axis_index("blk") * seq_size + lax.axis_index("seq")

time: 373 us -> 321 us (0.86)
  Pallas kernels: 342 us -> 293 us
  local copies, waits for them, and re-layouts: 21.8 us -> 15.3 us
    pallas_call x3 -> x1, Pallas kernels: 160 us -> 110 us  [forward(): pl.pallas_call(functools.partial(forward_kernel, grid, groups, tile_rows)...]
    squeeze x8 -> x0, local copies, waits for them, and re-layouts: 5.38 us -> none  [per_device(): bq, bv, bo, g1, s1, bd, g2, s2 = (vecs[i] for i in range(len(vectors)))]
where the time goes in v3:
time: 321 us; the launch traced here: 320 us
  Pallas kernels  293 us (91%)
  local copies, waits for them, and re-layouts  15.3 us (5%)
  other arithmetic  10.7 us (3%)
    pallas_call x1, Pallas kernels, backward(): pl.pallas_call(functools.partial(backward_kernel, grid, flat, len(bufs),...  160 us
    pallas_call x1, Pallas kernels, forward(): pl.pallas_call(functools.partial(forward_kernel, grid, groups, tile_rows)...  110 us
    pallas_call x1, Pallas kernels, contrast(): pl.pallas_call(functools.partial(contrast_kernel, grid), out_shape=[struc...  23.4 us

profile of v3, /device:TPU:0, one launch (start us, length us, event | category | flops | bytes accessed | tf_op | source)
XLA Modules:
  0.0 319.8 jit_solution(8049130393126764804)
XLA Ops:
  0.7 0.7 bitcast_convert_fusion.8
  2.0 0.7 reshape.154
  2.8 0.7 bitcast_convert_fusion.6
  3.5 0.7 bitcast_convert_fusion.4
  4.2 0.7 bitcast_convert_fusion
  4.9 0.7 bitcast_convert_fusion.2
  5.8 1.2 stack.87.refs_2_
  7.0 0.7 broadcast_in_dim.6.len_ref
  7.7 0.7 broadcast_in_dim.8.pair_ref
  9.0 0.7 fusion.1.refs_9_
  9.8 0.8 fusion.2.refs_12_
  10.5 1.0 fusion.refs_11_
  11.6 110.1 %shard_map.313 = (bf16[2,512,768]{2,1,0:T(8,128)(2,1)}, bf16[2,512,768]{2,1,0:T(8,128)(2,1)}, bf16[2,512,768]{2,1,0:T(8,128)(2,1)}, bf16[2,512,768]{2,1,0:T(8,12...) custom-call(s32[2,4]{1,0:T(2,128)} %copy-done.9, ...), custom_call_target="tpu_custom_call" | custom-call | tf_op jit(solution)/shard_map/pallas_call | solution.py:1116
  121.6 0.9 slice.60
  122.6 1.4 fusion.14
  124.1 0.7 reshape.156.pairs_ref
  124.7 23.4 %shard_map.314 = (f32[8,128]{1,0:T(8,128)}, bf16[128,768]{1,0:T(8,128)(2,1)}) custom-call(f32[8,768]{1,0:T(8,128)} %get-tuple-element.52.pool_ref, f32[8,128]{1,0:T(8,128)} %broadcast_in_dim.6.len_ref, s32[8,128]{1,0:T(8,128)} %broadcast_in_dim.8.pair_ref, s32[1,256]{1,0:T(1,128)} %reshape.156.pairs_ref), custom_call_target="tpu_custom_call" | custom-call | tf_op jit(solution)/shard_map/pallas_call | solution.py:612
  148.1 159.5 %shard_map.315 = (f32[24,3072]{1,0:T(8,128)}, f32[96,768]{1,0:T(8,128)}, f32[24,768]{1,0:T(8,128)}, f32[24,768]{1,0:T(8,128)}, f32[24,768]{1,0:T(8,128)}, /*inde...) custom-call(s32[2,4]{1,0:T(2,128)} %copy-done.9, ...), custom_call_target="tpu_custom_call" | custom-call | tf_op jit(solution)/shard_map/pallas_call | solution.py:1541
  308.5 0.7 slice.56
  309.2 0.7 slice.50
  311.2 3.5 %convert_element_type.66 = f32[8,128,768]{2,1,0:T(8,128)} convert(bf16[8,128,768]{2,1,0:T(8,128)(2,1)} %get-tuple-element.78) | non-fusion elementwise | flops 786432 | bytes 4718592 | tf_op jit(solution)/shard_map/convert_element_type | solution.py:1628
  314.7 1.1 copy.49
  318.4 0.7 copy.54
  319.1 0.7 copy.55
  (51 shorter events, 6.4 us)
Async XLA Ops:
  0.7 4.9 %copy-start = (s32[8,4]{0,1:T(4,128)S(1)}, s32[8,4]{0,1:T(4,128)}, u32[]{:S(2)}) copy-start(s32[8,4]{0,1:T(4,128)} %param.19) | copy-start | bytes 388
  5.7 5.9 %copy-start.9 = (s32[2,4]{1,0:T(2,128)}, s32[2,4]{1,0:T(2,128)S(1)}, u32[]{:S(2)}) copy-start(s32[2,4]{1,0:T(2,128)S(1)} %copy.40.refs_0_) | copy-start | bytes 100
  148.1 159.6 %copy-start.10 = (f32[8,128]{1,0:T(8,128)S(1)}, f32[8,128]{1,0:T(8,128)}, u32[]{:S(2)}) copy-start(f32[8,128]{1,0:T(8,128)} %get-tuple-element.77) | copy-start | bytes 12292
  311.2 3.5 %copy-start.2 = (bf16[8,128,768]{2,1,0:T(8,128)(2,1)S(1)}, bf16[8,128,768]{2,1,0:T(8,128)(2,1)}, u32[]{:S(2)}) copy-start(bf16[8,128,768]{2,1,0:T(8,128)(2,1)} %get-tuple-element.122) | copy-start | bytes 4718596
  314.6 1.2 copy-start.8
  314.6 1.8 copy-start.7
  314.6 2.5 copy-start.6
  314.6 3.1 copy-start.5
  314.7 3.7 %copy-start.4 = (f32[24,3072]{1,0:T(8,128)S(1)}, f32[24,3072]{1,0:T(8,128)}, u32[]{:S(2)}) copy-start(f32[24,3072]{1,0:T(8,128)} %get-tuple-element.134) | copy-start | bytes 884740
  314.7 4.4 %copy-start.3 = (f32[96,768]{1,0:T(8,128)S(1)}, f32[96,768]{1,0:T(8,128)}, u32[]{:S(2)}) copy-start(f32[96,768]{1,0:T(8,128)} %get-tuple-element.136) | copy-start | bytes 884740
  314.7 5.1 %copy-start.1 = (s32[8,4]{0,1:T(4,128)S(1)}, s32[8,4]{0,1:T(4,128)}, u32[]{:S(2)}) copy-start(s32[8,4]{0,1:T(4,128)} %param.19) | copy-start | bytes 388
